TPU v7x, 256 devices: a whole 4x4x8 slice. The times are simulated.
256 devices in a mesh: dp: 64 (over x, z, core), mp: 4 (over y).
Axes of the slice: x: 4, y: 4, z: 8, core: 2. Of those that a mesh axis runs over, the one named last changes fastest.
Arguments:
- descriptors: bfloat16 [262144, 1024], P(('dp', 'mp')), may hold values from -440 to 440
- database: bfloat16 [524288, 1024], P(('dp', 'mp')), may hold values from -80 to 80
- anchor_row: int32 [256, 64, 24], P(('dp', 'mp')), may hold values from 0 to 1023
- partner_row: int32 [256, 64, 24], P(('dp', 'mp')), may hold values from 0 to 1023
- block_counts: int32 [256, 64], P(('dp', 'mp')), may hold values from 1 to 24, 1024 in all within a row
Outputs:
- whitened: bfloat16 [524288, 1024], P(('dp', 'mp'))
Inputs may be any that keep to these rules, and one draw needn't show every extreme that they name: `block_counts`: the counts of one device add up to 1024; every device has a block with exactly 24 live pairs; slots from a block's count on are not pairs.
All inputs are finite; a program needn't handle non-finite values.
Results may differ from a plain program's by a relative error of at most 0.0015.
The roundings to bfloat16 on the way count: a program that leaves them out, or rounds other values in their place, can miss the bound.
Values may be sent and summed in bfloat16 or wider, within the bound.
A program may use at most 128 MiB of HBM per device.

v0:
```python
import jax
import jax.numpy as jnp
from jax import lax
from jax.sharding import PartitionSpec as P

PAIRS_DEV = 1024


shrink_weight = 0.5
ridge_term = 0.05
norm_epsilon = 1e-06
contract_rows = (((0,), (0,)), ((), ()))


def shards(descriptors, database, anchor_row, partner_row, block_counts):
    feature_width = descriptors.shape[1]
    local_rows = descriptors.shape[0]
    peer_count = partner_row.shape[1]
    slot_count = partner_row.shape[2]
    devices = lax.axis_size("dp") * lax.axis_size("mp")
    pairs_all = PAIRS_DEV * devices
    rows_all = local_rows * devices
    block_width = feature_width // lax.axis_size("mp")
    slot_iota = lax.broadcasted_iota(jnp.int32, (peer_count, slot_count), 1)
    live_slots = slot_iota < block_counts[0][:, None]
    anchors = jnp.take(descriptors, anchor_row[0].reshape(-1), axis=0).reshape(
        peer_count, slot_count, feature_width
    )
    requested = lax.all_to_all(partner_row[0], "dp", split_axis=0, concat_axis=0, tiled=True)
    found_rows = jnp.take(descriptors, requested.reshape(-1), axis=0)
    found_rows = found_rows.reshape(requested.shape + (feature_width,))
    partners = lax.all_to_all(found_rows, "dp", split_axis=0, concat_axis=0, tiled=True)
    differences = jnp.where(
        live_slots[:, :, None], anchors.astype(jnp.float32) - partners.astype(jnp.float32), 0.0
    )
    pair_flat = differences.astype(jnp.bfloat16).reshape(-1, feature_width)
    col_sum = jnp.sum(descriptors, axis=0, dtype=jnp.float32)
    pair_gram = lax.dot_general(
        pair_flat, pair_flat, contract_rows, preferred_element_type=jnp.float32
    )
    row_gram = lax.dot_general(
        descriptors, descriptors, contract_rows, preferred_element_type=jnp.float32
    )
    partial_sum = pair_gram * (1.0 / pairs_all) + row_gram * (shrink_weight / rows_all)
    summed, col_total = lax.psum((partial_sum, col_sum), ("dp", "mp"))
    col_mean = col_total / rows_all
    identity = jnp.eye(feature_width, dtype=jnp.float32)
    metric = summed - shrink_weight * col_mean[:, None] * col_mean[None, :] + ridge_term * identity
    factor = jnp.linalg.cholesky(metric)
    mp_index = lax.axis_index("mp")
    row_iota = lax.broadcasted_iota(jnp.int32, (feature_width, block_width), 0)
    col_iota = lax.broadcasted_iota(jnp.int32, (feature_width, block_width), 1)
    unit_cols = (row_iota == col_iota + mp_index * block_width).astype(jnp.float32)
    inverse_cols = lax.linalg.triangular_solve(
        factor, unit_cols, left_side=True, lower=True, transpose_a=True
    ).astype(jnp.bfloat16)
    centered = (database.astype(jnp.float32) - col_mean).astype(jnp.bfloat16)
    projected = jnp.dot(
        centered,
        lax.all_gather(inverse_cols, "mp", axis=1, tiled=True),
        preferred_element_type=jnp.float32,
    )
    row_scale = lax.rsqrt(jnp.mean(projected * projected, axis=1, keepdims=True) + norm_epsilon)
    return (projected * row_scale).astype(jnp.bfloat16)


def solution(mesh):
    placed = (
        P(("dp", "mp"), None),
        P(("dp", "mp"), None),
        P(("dp", "mp"), None, None),
        P(("dp", "mp"), None, None),
        P(("dp", "mp"), None),
    )
    return jax.shard_map(
        shards, mesh=mesh, in_specs=placed, out_specs=P(("dp", "mp"), None), check_vma=False
    )
```

profile of v0, /device:TPU:1, one launch (start us, length us, event | category | flops | bytes accessed | tf_op | source)
XLA Modules:
  0.0 804.6 jit_solution(3194894882853169398)
XLA Ops:
  7.9 13.0 %all-to-all-start = ((s32[64,1,24]{2,1,0:T(1,128)}), s32[64,1,24]{2,1,0:T(1,128)S(1)}, u32[]{:S(2)}, u32[]{:S(2)}) async-start(s32[64,1,24]{2,1,0:T(1,128)} %bitcast.2), calls=%async_computation | async-start | bytes 65536 | tf_op jit(solution)/shard_map/all_to_all | solution.py:29
  31.5 9.0 %gather_fusion.1 = bf16[1536,1024]{1,0:T(8,128)(2,1)S(1)} fusion(bf16[1024,1024]{1,0:T(8,128)(2,1)} %param.7, s32[2048]{0:T(1024)S(1)} %get-tuple-element.62), kind=kCustom, calls=%fused_computation.1.clone | custom fusion | bytes 6297600 | tf_op jit(solution)/shard_map/jit(_take)/gather | solution.py:30
  58.0 63.9 %all-to-all-done.1 = bf16[64,24,1024]{2,1,0:T(8,128)(2,1)} async-done(((bf16[64,24,1024]{2,1,0:T(8,128)(2,1)}), bf16[64,24,1024]{2,1,0:T(8,128)(2,1)}, u32[]{:S(2)}, u32[]{:S(2)}) %all-to-all-start.1) | async-done | bytes 3145760 | tf_op jit(solution)/shard_map/all_to_all | solution.py:32
  121.9 8.7 %fusion.6 = f32[1024,1024,1]{0,1,2:T(8,128)S(1)} fusion(bf16[64,24,1024]{2,1,0:T(8,128)(2,1)} %bitcast.104, bf16[64,24,1024]{2,1,0:T(8,128)(2,1)} %all-to-all-done.1, pred[64,24]{1,0:T(8,128)(4,1)S(1)} %iota_compare_fusion.5), kind=kOutput, calls=%fused_computation.21 | convolution fusion | flops 3229089792 | bytes 10487296 | tf_op jit(solution)/shard_map/dot_general | solution.py:38
  135.7 76.9 %psum.14 = f32[1024]{0:T(1024)S(1)} all-reduce(f32[1024]{0:T(1024)S(1)} %convert_reduce_fusion), channel_id=1, replica_groups=mesh['dp'=64,'mp'=4] {'dp','mp'}, use_global_device_ids=true, to_apply=%region_1.2 | all-reduce | flops 1024 | bytes 8192 | tf_op jit(solution)/shard_map/psum | solution.py:45
  212.9 186.8 %all-reduce.3.cloned.1.call-done = f32[1024,1024]{0,1:T(8,128)} async-done(((f32[1024,1024]{0,1:T(8,128)}), f32[1024,1024]{0,1:T(8,128)}) %all-reduce.3.cloned.1.call-update) | async-done | bytes 4194320 | tf_op jit(solution)/shard_map/psum | solution.py:45
  416.0 11.7 %cholesky.222 = f32[128,128]{1,0:T(8,128)S(1)} custom-call(f32[128,128]{1,0:T(8,128)S(1)} %cholesky.577), custom_call_target="Cholesky" | custom-call | tf_op jit(solution)/shard_map/jit(cholesky)/cholesky | solution.py:49
  427.7 9.8 %custom-call.62 = f32[1,128,128]{1,2,0:T(8,128)S(1)} custom-call(f32[1,128,128]{2,1,0:T(8,128)S(1)} %get-tuple-element.49), custom_call_target="InvertDiagBlocksLowerTriangular" | custom-call | tf_op jit(solution)/shard_map/jit(cholesky)/cholesky | solution.py:49
  441.0 11.7 %cholesky.243 = f32[128,128]{1,0:T(8,128)S(1)} custom-call(f32[128,128]{1,0:T(8,128)S(1)} %cholesky.581), custom_call_target="Cholesky" | custom-call | tf_op jit(solution)/shard_map/jit(cholesky)/cholesky | solution.py:49
  452.8 10.2 %custom-call.63 = f32[1,128,128]{1,2,0:T(8,128)S(1)} custom-call(f32[1,128,128]{2,1,0:T(8,128)S(1)} %get-tuple-element.47), custom_call_target="InvertDiagBlocksLowerTriangular" | custom-call | tf_op jit(solution)/shard_map/jit(cholesky)/cholesky | solution.py:49
  468.5 11.7 %cholesky.466 = f32[128,128]{1,0:T(8,128)S(1)} custom-call(f32[128,128]{1,0:T(8,128)S(1)} %cholesky.586), custom_call_target="Cholesky" | custom-call | tf_op jit(solution)/shard_map/jit(cholesky)/cholesky | solution.py:49
  481.0 9.8 %custom-call.64 = f32[1,128,128]{1,2,0:T(8,128)S(1)} custom-call(f32[1,128,128]{2,1,0:T(8,128)S(1)} %get-tuple-element.45), custom_call_target="InvertDiagBlocksLowerTriangular" | custom-call | tf_op jit(solution)/shard_map/jit(cholesky)/cholesky | solution.py:49
  495.3 11.7 %cholesky.485 = f32[128,128]{1,0:T(8,128)S(1)} custom-call(f32[128,128]{1,0:T(8,128)S(1)} %cholesky.591), custom_call_target="Cholesky" | custom-call | tf_op jit(solution)/shard_map/jit(cholesky)/cholesky | solution.py:49
  507.8 9.8 %custom-call.65 = f32[1,128,128]{1,2,0:T(8,128)S(1)} custom-call(f32[1,128,128]{2,1,0:T(8,128)S(1)} %get-tuple-element.43), custom_call_target="InvertDiagBlocksLowerTriangular" | custom-call | tf_op jit(solution)/shard_map/jit(cholesky)/cholesky | solution.py:49
  521.9 11.7 %cholesky.504 = f32[128,128]{1,0:T(8,128)S(1)} custom-call(f32[128,128]{1,0:T(8,128)S(1)} %cholesky.596), custom_call_target="Cholesky" | custom-call | tf_op jit(solution)/shard_map/jit(cholesky)/cholesky | solution.py:49
  534.4 10.0 %custom-call.66 = f32[1,128,128]{1,2,0:T(8,128)S(1)} custom-call(f32[1,128,128]{2,1,0:T(8,128)S(1)} %get-tuple-element.41), custom_call_target="InvertDiagBlocksLowerTriangular" | custom-call | tf_op jit(solution)/shard_map/jit(cholesky)/cholesky | solution.py:49
  548.6 11.7 %cholesky.524 = f32[128,128]{1,0:T(8,128)S(1)} custom-call(f32[128,128]{1,0:T(8,128)S(1)} %cholesky.601), custom_call_target="Cholesky" | custom-call | tf_op jit(solution)/shard_map/jit(cholesky)/cholesky | solution.py:49
  561.1 9.8 %custom-call.67 = f32[1,128,128]{1,2,0:T(8,128)S(1)} custom-call(f32[1,128,128]{2,1,0:T(8,128)S(1)} %get-tuple-element.39), custom_call_target="InvertDiagBlocksLowerTriangular" | custom-call | tf_op jit(solution)/shard_map/jit(cholesky)/cholesky | solution.py:49
  574.6 12.1 %cholesky.544 = f32[128,128]{1,0:T(8,128)S(1)} custom-call(f32[128,128]{1,0:T(8,128)S(1)} %cholesky.606), custom_call_target="Cholesky" | custom-call | tf_op jit(solution)/shard_map/jit(cholesky)/cholesky | solution.py:49
  587.5 9.8 %custom-call.68 = f32[1,128,128]{1,2,0:T(8,128)S(1)} custom-call(f32[1,128,128]{2,1,0:T(8,128)S(1)} %get-tuple-element.37), custom_call_target="InvertDiagBlocksLowerTriangular" | custom-call | tf_op jit(solution)/shard_map/jit(cholesky)/cholesky | solution.py:49
  600.3 11.7 %cholesky.562 = f32[128,128]{1,0:T(8,128)S(1)} custom-call(f32[128,128]{1,0:T(8,128)S(1)} %convolution_subtract_fusion.13), custom_call_target="Cholesky" | custom-call | tf_op jit(solution)/shard_map/jit(cholesky)/cholesky | solution.py:49
  628.0 24.4 %while.1 = (s32[]{:T(128)}, f32[1024,1024]{0,1:T(8,128)}, s32[8,2]{0,1:T(2,128)S(1)}, f32[8,128,128]{2,1,0:T(8,128)S(1)}, s32[]{:T(128)}) while((s32[]{:T(128)}, f32[1024,1024]{0,1:T(8,128)}, s32[8,2]{0,1:T(2,128)S(1)}, f32[8,128,128]{2,1,0:T(8,128)S(1)}, s32[]{:T(128)}) %tuple.38), condition=%wide.while_cond, body=%wide.while_body.sunk | while | flops 2 | bytes 393321 | solution.py:54
  652.4 78.8 %custom-call.69 = f32[8,128,128]{1,2,0:T(8,128)S(1)} custom-call(f32[8,128,128]{2,1,0:T(8,128)S(1)} %get-tuple-element.13), custom_call_target="InvertDiagBlocksLowerTriangular" | custom-call | tf_op jit(solution)/shard_map/triangular_solve | solution.py:54
  744.1 36.7 %all-gather.2.cloned.1.call-done = bf16[1024,1024]{1,0:T(8,128)(2,1)} async-done(((bf16[1024,256]{1,0:T(8,128)(2,1)}), bf16[1024,1024]{1,0:T(8,128)(2,1)}) %all-gather.2.cloned.1.call-update) | async-done | bytes 2097168 | tf_op jit(solution)/shard_map/all_gather | solution.py:60
  (179 shorter events, 148.2 us)
Async XLA Ops:
  7.9 22.2 %all-to-all-start = ((s32[64,1,24]{2,1,0:T(1,128)}), s32[64,1,24]{2,1,0:T(1,128)S(1)}, u32[]{:S(2)}, u32[]{:S(2)}) async-start(s32[64,1,24]{2,1,0:T(1,128)} %bitcast.2), calls=%async_computation | async-start | bytes 65536 | tf_op jit(solution)/shard_map/all_to_all | solution.py:29
  42.7 6.0 copy-start.4
  42.7 6.1 copy-start
  42.7 79.2 %all-to-all-start.1 = ((bf16[64,24,1024]{2,1,0:T(8,128)(2,1)}), bf16[64,24,1024]{2,1,0:T(8,128)(2,1)}, u32[]{:S(2)}, u32[]{:S(2)}) async-start(bf16[64,24,1024]{2,1,0:T(8,128)(2,1)} %bitcast.103), calls=%async_computation.1 | async-start | bytes 6291456 | tf_op jit(solution)/shard_map/all_to_all | solution.py:32
  48.4 351.2 %all-reduce.3.cloned.1.call-start = ((), (), s32[]{:S(2)}) async-start(), calls=%async_computation.2 | async-start | bytes 8388608 | tf_op jit(solution)/shard_map/psum | solution.py:45
  135.3 645.5 %all-gather.2.cloned.1.call-start = ((), (), s32[]{:S(2)}) async-start(), calls=%async_computation.3 | async-start | bytes 2621440 | tf_op jit(solution)/shard_map/all_gather | solution.py:60
  414.0 2.0 copy-start.2
  464.1 1.9 copy-start.1
  743.3 0.8 copy-start.3
Sparse Core Ops, SparseCore 0:
  135.4 264.1 all-reduce.2
  744.3 36.4 all-gather.1
where the time goes:
time: 810 us; the launch traced here: 805 us
  waiting for transfers between devices  296 us (37%)
  other arithmetic  272 us (34%)
  blocking collectives  76.9 us (9%)
  local copies, waits for them, and re-layouts  64 us (8%)
  matrix products  57.9 us (7%)
  between operations  19.3 us (2%)
  starting transfers between devices  19 us (2%)
    psum x1, waiting for transfers between devices, shards(): summed, col_total = lax.psum((partial_sum, col_sum), ('dp', 'mp'))  187 us
    another operation x31, other arithmetic, shards(): factor = jnp.linalg.cholesky(metric)  169 us
    another operation x4, other arithmetic, shards(): lax.linalg.triangular_solve(factor, unit_cols, left_side=True, lower=True...  83.7 us
    psum x1, blocking collectives, shards(): summed, col_total = lax.psum((partial_sum, col_sum), ('dp', 'mp'))  76.9 us
    all_to_all x1, waiting for transfers between devices, shards(): lax.all_to_all(found_rows, 'dp', split_axis=0, concat_axis=0, tiled=True)  63.9 us
    all_gather x1, waiting for transfers between devices, shards(): lax.all_gather(inverse_cols, 'mp', axis=1, tiled=True)  36.7 us
    another operation x14, matrix products, shards(): factor = jnp.linalg.cholesky(metric)  25.7 us
    another operation x40, local copies, waits for them, and re-layouts  24.1 us
  transfers between devices with their start and end apart: 4, of which 4 were waited for; matrix products, arithmetic and copies ran while one was open for 1% of the time, Pallas kernels for 0%

commit v1 on v0

v1 whole, which is shorter than its diff:
```python
import jax
import jax.numpy as jnp
from jax import lax
from jax.experimental import pallas as pl
from jax.experimental.pallas import tpu as pltpu
from jax.sharding import PartitionSpec as P

PAIRS_DEV = 1024


shrink_weight = 0.5
ridge_term = 0.05
norm_epsilon = 1e-06
contract_rows = (((0,), (0,)), ((), ()))

N = 1024
NB = 128
F32 = jnp.float32
HI = lax.Precision.HIGHEST

def lane_bcast(x, c):
    return jnp.broadcast_to(x[:, c:c + 1], x.shape)

def row_bcast(x, i):
    return jnp.broadcast_to(x[i:i + 1, :], x.shape)

def factor_block(rows):
    lane = lax.broadcasted_iota(jnp.int32, (8, NB), 1)
    count = len(rows)
    for q in range(count):
        base = 8 * q
        inside = (lane >= base) & (lane < base + 8)
        cur = rows[q]
        cols = [lane_bcast(cur, base + j) for j in range(8)]
        d = {}
        for j in range(8):
            for i in range(j, 8):
                d[i, j] = row_bcast(cols[j], i)
        w = [jnp.where(inside, jnp.where(lane == base + i, 1.0, 0.0), row_bcast(cur, i)) for i in range(8)]
        inv, l, rs = [], {}, []
        for j in range(8):
            p = d[j, j]
            r = 1.0 / p
            inv.append(r)
            rs.append(lax.rsqrt(p))
            for i in range(j + 1, 8):
                l[i, j] = d[i, j] * r
            for i in range(j + 1, 8):
                for k in range(j + 1, i + 1):
                    d[i, k] = d[i, k] - l[i, j] * d[k, j]
            for i in range(j + 1, 8):
                w[i] = w[i] - l[i, j] * w[j]
        g = [None] * 8
        for i in range(7, -1, -1):
            acc = inv[i] * w[i]
            for j in range(i + 1, 8):
                acc = acc - l[j, i] * g[j]
            g[i] = acc
        sub = lax.broadcasted_iota(jnp.int32, (8, NB), 0)
        out = rs[0] * w[0]
        for i in range(1, 8):
            out = jnp.where(sub == i, rs[i] * w[i], out)
        rows[q] = out
        for t in range(q + 1, count):
            acc = jnp.where(inside, 0.0, rows[t])
            for j in range(8):
                acc = acc - lane_bcast(rows[t], base + j) * g[j]
            rows[t] = acc
    return rows

def chol_kernel(m_ref, out_ref, c_ref, t_ref):
    c_ref[...] = m_ref[...]
    blocks = N // NB
    row = lax.broadcasted_iota(jnp.int32, (NB, NB), 0)
    col = lax.broadcasted_iota(jnp.int32, (NB, NB), 1)

    def step(k, _):
        off = pl.multiple_of(k * NB, NB)
        diag = c_ref.at[pl.ds(off, NB), pl.ds(off, NB)]
        rows = [diag[8 * q:8 * q + 8, :] for q in range(16)]
        rows = factor_block(rows)
        for q in range(16):
            t_ref[8 * q:8 * q + 8, :] = rows[q]
        t = jnp.where(row >= col, t_ref[...], 0.0)
        ck = jnp.dot(t, c_ref[pl.ds(off, NB), :], precision=HI, preferred_element_type=F32)
        c_ref[pl.ds(off, NB), :] = ck
        c_ref[pl.ds(off, NB), pl.ds(off, NB)] = t

        def update(i, _):
            io = pl.multiple_of(i * NB, NB)
            u = c_ref[pl.ds(off, NB), pl.ds(io, NB)]
            c_ref[pl.ds(io, NB), pl.ds(off, NB)] = jnp.zeros((NB, NB), F32)
            prod = lax.dot_general(u, c_ref[pl.ds(off, NB), :], (((0,), (0,)), ((), ())),
                                   precision=HI, preferred_element_type=F32)
            c_ref[pl.ds(io, NB), :] = c_ref[pl.ds(io, NB), :] - prod
            return 0
        lax.fori_loop(k + 1, blocks, update, 0)
        return 0
    lax.fori_loop(0, blocks, step, 0)
    for i in range(blocks):
        r = lax.broadcasted_iota(jnp.int32, (NB, N), 0) + i * NB
        c = lax.broadcasted_iota(jnp.int32, (NB, N), 1)
        out_ref[i * NB:(i + 1) * NB, :] = jnp.where(r >= c, c_ref[i * NB:(i + 1) * NB, :], 0.0).astype(out_ref.dtype)


def inverse_factor(metric):
    return pl.pallas_call(
        chol_kernel,
        out_shape=jax.ShapeDtypeStruct((N, N), jnp.bfloat16),
        in_specs=[pl.BlockSpec(memory_space=pltpu.VMEM)],
        out_specs=pl.BlockSpec(memory_space=pltpu.VMEM),
        scratch_shapes=[pltpu.VMEM((N, N), F32), pltpu.VMEM((NB, NB), F32)],
        compiler_params=pltpu.CompilerParams(vmem_limit_bytes=40 << 20),
    )(metric)


def whiten_kernel(db_ref, mean_ref, inv_ref, out_ref):
    centered = (db_ref[...].astype(F32) - mean_ref[0:1, :]).astype(jnp.bfloat16)
    projected = lax.dot_general(
        centered, inv_ref[...], (((1,), (1,)), ((), ())), preferred_element_type=F32
    )
    energy = jnp.mean(projected * projected, axis=1, keepdims=True)
    out_ref[...] = (projected * lax.rsqrt(energy + norm_epsilon)).astype(jnp.bfloat16)


def whiten(database, col_mean, inverse):
    rows, width = database.shape
    tile = 256
    return pl.pallas_call(
        whiten_kernel,
        grid=(rows // tile,),
        out_shape=jax.ShapeDtypeStruct((rows, width), jnp.bfloat16),
        in_specs=[
            pl.BlockSpec((tile, width), lambda i: (i, 0)),
            pl.BlockSpec((8, width), lambda i: (0, 0)),
            pl.BlockSpec((width, width), lambda i: (0, 0)),
        ],
        out_specs=pl.BlockSpec((tile, width), lambda i: (i, 0)),
        compiler_params=pltpu.CompilerParams(vmem_limit_bytes=40 << 20),
    )(database, jnp.broadcast_to(col_mean[None, :], (8, width)), inverse)


def shards(descriptors, database, anchor_row, partner_row, block_counts):
    feature_width = descriptors.shape[1]
    local_rows = descriptors.shape[0]
    peer_count = partner_row.shape[1]
    slot_count = partner_row.shape[2]
    devices = lax.axis_size("dp") * lax.axis_size("mp")
    pairs_all = PAIRS_DEV * devices
    rows_all = local_rows * devices
    slot_iota = lax.broadcasted_iota(jnp.int32, (peer_count, slot_count), 1)
    live_slots = slot_iota < block_counts[0][:, None]
    wanted = jnp.where(live_slots, partner_row[0], -1)
    anchors = descriptors.at[anchor_row[0].reshape(-1)].get(mode="promise_in_bounds").reshape(
        peer_count, slot_count, feature_width
    )
    wanted_here = lax.all_to_all(wanted, "dp", split_axis=0, concat_axis=0, tiled=True)
    anchors_here = lax.all_to_all(anchors, "dp", split_axis=0, concat_axis=0, tiled=True)
    partners = descriptors.at[jnp.maximum(wanted_here, 0).reshape(-1)].get(
        mode="promise_in_bounds"
    ).reshape(peer_count, slot_count, feature_width)
    differences = jnp.where(
        wanted_here[:, :, None] >= 0, anchors_here.astype(F32) - partners.astype(F32), 0.0
    )
    pair_flat = differences.astype(jnp.bfloat16).reshape(-1, feature_width)
    col_sum = jnp.sum(descriptors, axis=0, dtype=F32)
    pair_gram = lax.dot_general(pair_flat, pair_flat, contract_rows, preferred_element_type=F32)
    row_gram = lax.dot_general(
        descriptors, descriptors, contract_rows, preferred_element_type=F32
    )
    partial_sum = pair_gram * (1.0 / pairs_all) + row_gram * (shrink_weight / rows_all)
    summed, col_total = lax.psum((partial_sum, col_sum), ("dp", "mp"))
    col_mean = col_total / rows_all
    identity = jnp.eye(feature_width, dtype=F32)
    metric = summed - shrink_weight * col_mean[:, None] * col_mean[None, :] + ridge_term * identity
    return whiten(database, col_mean, inverse_factor(metric))


def solution(mesh):
    placed = (
        P(("dp", "mp"), None),
        P(("dp", "mp"), None),
        P(("dp", "mp"), None, None),
        P(("dp", "mp"), None, None),
        P(("dp", "mp"), None),
    )
    return jax.shard_map(
        shards, mesh=mesh, in_specs=placed, out_specs=P(("dp", "mp"), None), check_vma=False
    )
```

time: 810 us -> 484 us (0.60)
  other arithmetic: 272 us -> 4.44 us
  Pallas kernels: 0 us -> 78.7 us
  local copies, waits for them, and re-layouts: 64 us -> 17.5 us
  matrix products: 57.9 us -> 13.4 us
  waiting for transfers between devices: 296 us -> 254 us
    another operation x35 -> x0, other arithmetic: 253 us -> none  [the longest x31 169 us: shards(): factor = jnp.linalg.cholesky(metric)]
    pallas_call x0 -> x2, Pallas kernels: none -> 78.7 us  [the longest x1 71 us: inverse_factor(): pl.pallas_call(chol_kernel, out_shape=jax.ShapeDtypeStruct((N, N), jnp.bf...]
    another operation x29 -> x0, matrix products: 37.3 us -> none  [the longest x14 25.7 us: shards(): factor = jnp.linalg.cholesky(metric)]
    all_gather x1 -> x0, waiting for transfers between devices: 36.7 us -> none  [shards(): lax.all_gather(inverse_cols, 'mp', axis=1, tiled=True)]
    another operation x69 -> x0, local copies, waits for them, and re-layouts: 29.6 us -> none
  transfers between devices with their start and end apart: 4 -> 3, of which waited for: 4 -> 2; matrix products, arithmetic and copies ran while one was open for 1% -> 4% of each run, Pallas kernels for 0% -> 0%
where the time goes in v1:
time: 484 us; the launch traced here: 482 us
  waiting for transfers between devices  254 us (52%)
  Pallas kernels  78.7 us (16%)
  blocking collectives  77 us (16%)
  starting transfers between devices  23.6 us (5%)
  local copies, waits for them, and re-layouts  17.5 us (4%)
  between operations  13.5 us (3%)
  matrix products  13.4 us (3%)
    psum x1, waiting for transfers between devices, shards(): summed, col_total = lax.psum((partial_sum, col_sum), ('dp', 'mp'))  187 us
    psum x1, blocking collectives, shards(): summed, col_total = lax.psum((partial_sum, col_sum), ('dp', 'mp'))  77 us
    pallas_call x1, Pallas kernels, inverse_factor(): pl.pallas_call(chol_kernel, out_shape=jax.ShapeDtypeStruct((N, N), jnp.bf...  71 us
    all_to_all x1, waiting for transfers between devices, shards(): lax.all_to_all(anchors, 'dp', split_axis=0, concat_axis=0, tiled=True)  67.2 us
    all_to_all x1, starting transfers between devices, shards(): lax.all_to_all(wanted, 'dp', split_axis=0, concat_axis=0, tiled=True)  13 us
    all_to_all x1, starting transfers between devices, shards(): lax.all_to_all(anchors, 'dp', split_axis=0, concat_axis=0, tiled=True)  10.6 us
  transfers between devices with their start and end apart: 3, of which 2 were waited for; matrix products, arithmetic and copies ran while one was open for 4% of the time, Pallas kernels for 0%

profile of v1, /device:TPU:1, one launch (start us, length us, event | category | flops | bytes accessed | tf_op | source)
XLA Modules:
  0.0 482.3 jit_solution(15209161873768559293)
XLA Ops:
  6.5 0.8 copy.16
  7.3 1.4 compare_select_fusion
  8.7 13.0 %all-to-all-start = ((s32[64,1,24]{2,1,0:T(1,128)}), s32[64,1,24]{2,1,0:T(1,128)S(1)}, u32[]{:S(2)}, u32[]{:S(2)}) async-start(s32[64,1,24]{2,1,0:T(1,128)} %compare_select_fusion), calls=%async_computation | async-start | bytes 65536 | tf_op jit(solution)/shard_map/all_to_all | solution.py:157
  21.7 0.8 copy.19
  22.5 0.1 reshape_squeeze.3
  22.7 9.7 %gather_fusion = bf16[1536,1024]{1,0:T(8,128)(2,1)} fusion(bf16[1024,1024]{1,0:T(8,128)(2,1)} %param.5, s32[2048]{0:T(1024)S(1)} %pad_clamp_fusion.1), kind=kCustom, calls=%fused_computation | custom fusion | bytes 6297600 | tf_op jit(solution)/shard_map/gather | solution.py:154
  32.3 10.6 %all-to-all-start.1 = ((bf16[64,24,1024]{2,1,0:T(8,128)(2,1)}), bf16[64,24,1024]{2,1,0:T(8,128)(2,1)}, u32[]{:S(2)}, u32[]{:S(2)}) async-start(bf16[64,24,1024]{2,1,0:T(8,128)(2,1)} %bitcast.15), calls=%async_computation.1 | async-start | bytes 6291456 | tf_op jit(solution)/shard_map/all_to_all | solution.py:158
  42.9 0.0 all-reduce.2.cloned.1.call-start
  43.0 0.1 copy.17
  43.1 0.1 copy.21
  43.1 0.1 reshape.120
  43.3 5.8 %gather_fusion.1 = bf16[1536,1024]{1,0:T(8,128)(2,1)} fusion(bf16[1024,1024]{1,0:T(8,128)(2,1)S(1)} %copy-done.1, s32[2048]{0:T(1024)S(1)} %pad_clamp_fusion), kind=kCustom, calls=%fused_computation.1 | custom fusion | bytes 6297600 | tf_op jit(solution)/shard_map/gather | solution.py:159
  49.1 0.1 copy.18
  49.2 67.2 %all-to-all-done.1 = bf16[64,24,1024]{2,1,0:T(8,128)(2,1)} async-done(((bf16[64,24,1024]{2,1,0:T(8,128)(2,1)}), bf16[64,24,1024]{2,1,0:T(8,128)(2,1)}, u32[]{:S(2)}, u32[]{:S(2)}) %all-to-all-start.1) | async-done | bytes 3145760 | tf_op jit(solution)/shard_map/all_to_all | solution.py:158
  116.4 9.0 %fusion.3 = f32[1024,1024,1]{1,0,2:T(8,128)S(1)} fusion(bf16[64,24,1024]{2,1,0:T(8,128)(2,1)} %bitcast.16, bf16[64,24,1024]{2,1,0:T(8,128)(2,1)} %all-to-all-done.1, pred[64,24]{1,0:T(8,128)(4,1)S(1)} %copy.18), kind=kOutput, calls=%fused_computation.10 | convolution fusion | flops 3229089792 | bytes 10487296 | tf_op jit(solution)/shard_map/dot_general | solution.py:167
  125.4 4.5 fusion.2
  129.8 0.0 all-reduce.2.cloned.1.call-update
  129.8 0.4 convert_reduce_fusion
  130.2 77.0 %psum.14 = f32[1024]{0:T(1024)S(1)} all-reduce(f32[1024]{0:T(1024)S(1)} %convert_reduce_fusion), channel_id=1, replica_groups=mesh['dp'=64,'mp'=4] {'dp','mp'}, use_global_device_ids=true, to_apply=%region_1.2 | all-reduce | flops 1024 | bytes 8192 | tf_op jit(solution)/shard_map/psum | solution.py:172
  207.2 186.9 %all-reduce.2.cloned.1.call-done = f32[1024,1024]{1,0:T(8,128)} async-done(((f32[1024,1024]{1,0:T(8,128)}), f32[1024,1024]{1,0:T(8,128)}) %all-reduce.2.cloned.1.call-update) | async-done | bytes 4194320 | tf_op jit(solution)/shard_map/psum | solution.py:172
  394.1 2.6 select_add_fusion.m_ref
  396.7 0.0 copy-start
  396.8 71.0 %shard_map.55.inv_ref = bf16[1024,1024]{1,0:T(8,128)(2,1)S(1)} custom-call(f32[1024,1024]{1,0:T(8,128)S(1)} %select_add_fusion.m_ref), custom_call_target="tpu_custom_call" | custom-call | tf_op jit(solution)/shard_map/pallas_call | solution.py:107
  467.8 7.6 %shard_map.56 = bf16[2048,1024]{1,0:T(8,128)(2,1)} custom-call(bf16[2048,1024]{1,0:T(8,128)(2,1)S(1)} %copy-done, f32[8,1024]{1,0:T(8,128)S(1)} %broadcast_in_dim.18.mean_ref, bf16[1024,1024]{1,0:T(8,128)(2,1)S(1)} %shard_map.55.inv_ref), custom_call_target="tpu_custom_call" | custom-call | tf_op jit(solution)/shard_map/pallas_call | solution.py:129
  (11 shorter events, 0.1 us)
Async XLA Ops:
  8.7 23.6 %all-to-all-start = ((s32[64,1,24]{2,1,0:T(1,128)}), s32[64,1,24]{2,1,0:T(1,128)S(1)}, u32[]{:S(2)}, u32[]{:S(2)}) async-start(s32[64,1,24]{2,1,0:T(1,128)} %compare_select_fusion), calls=%async_computation | async-start | bytes 65536 | tf_op jit(solution)/shard_map/all_to_all | solution.py:157
  32.3 11.0 %copy-start.1 = (bf16[1024,1024]{1,0:T(8,128)(2,1)S(1)}, bf16[1024,1024]{1,0:T(8,128)(2,1)}, u32[]{:S(2)}) copy-start(bf16[1024,1024]{1,0:T(8,128)(2,1)} %param.5) | copy-start | bytes 6291460
  32.3 84.1 %all-to-all-start.1 = ((bf16[64,24,1024]{2,1,0:T(8,128)(2,1)}), bf16[64,24,1024]{2,1,0:T(8,128)(2,1)}, u32[]{:S(2)}, u32[]{:S(2)}) async-start(bf16[64,24,1024]{2,1,0:T(8,128)(2,1)} %bitcast.15), calls=%async_computation.1 | async-start | bytes 6291456 | tf_op jit(solution)/shard_map/all_to_all | solution.py:158
  42.9 351.2 %all-reduce.2.cloned.1.call-start = ((), (), s32[]{:S(2)}) async-start(), calls=%async_computation.2 | async-start | bytes 8388608 | tf_op jit(solution)/shard_map/psum | solution.py:172
  396.7 71.1 %copy-start = (bf16[2048,1024]{1,0:T(8,128)(2,1)S(1)}, bf16[2048,1024]{1,0:T(8,128)(2,1)}, u32[]{:S(2)}) copy-start(bf16[2048,1024]{1,0:T(8,128)(2,1)} %db_ref.1) | copy-start | bytes 12582916
Sparse Core Ops, SparseCore 0:
  130.0 264.1 all-reduce.1

commit v2 on v1

--- a/solution.py
+++ b/solution.py
@@ -6,6 +6,7 @@
 from jax.sharding import PartitionSpec as P
 
 PAIRS_DEV = 1024
+R_ALL = 262144
 
 
 shrink_weight = 0.5
@@ -68,11 +69,240 @@
             rows[t] = acc
     return rows
 
-def chol_kernel(m_ref, out_ref, c_ref, t_ref):
-    c_ref[...] = m_ref[...]
-    blocks = N // NB
+
+NX, NY, NZ, NC = 4, 4, 8, 2
+PLANE = NX * NY
+BLOCKS = N // NB
+UPPER = [(i, j) for i in range(BLOCKS) for j in range(i, BLOCKS)]
+DATA = len(UPPER) * NB // (NC * PLANE)
+UNIT = DATA + 8
+HALF = PLANE * UNIT
+PIECE = 24
+SEG = 16
+
+
+def segments():
+    found = []
+    for b, (i, j) in enumerate(UPPER):
+        for s in range(0, NB, SEG):
+            flat = b * NB + s
+            unit, inside = flat // DATA, flat % DATA
+            found.append((i, j, s, unit * UNIT + inside))
+    return found
+
+
+def gram_kernel(pair_scale, row_scale, here_ref, part_ref, live_ref, desc_ref, out_ref, diff_ref, gram_ref):
+    slots = here_ref.shape[0]
+    tile = 256
+    for r in range(0, slots, tile):
+        gap = here_ref[r:r + tile, :].astype(F32) - part_ref[r:r + tile, :].astype(F32)
+        keep = jnp.broadcast_to(live_ref[r:r + tile, 0:1], gap.shape)
+        diff_ref[r:r + tile, :] = jnp.where(keep > 0.5, gap, 0.0).astype(jnp.bfloat16)
+    for i in range(0, N, tile):
+        pair = lax.dot_general(diff_ref[:, i:i + tile], diff_ref[:, i:], contract_rows, preferred_element_type=F32)
+        row = lax.dot_general(desc_ref[:, i:i + tile], desc_ref[:, i:], contract_rows, preferred_element_type=F32)
+        gram_ref[i:i + tile, i:] = pair * pair_scale + row * row_scale
+    for i, j, s, at in segments():
+        out_ref[at:at + SEG, :] = gram_ref[i * NB + s:i * NB + s + SEG, j * NB:(j + 1) * NB]
+    ones = jnp.ones((8, desc_ref.shape[0]), jnp.bfloat16)
+    sums = jnp.dot(ones, desc_ref[...], preferred_element_type=F32)
+    sub = lax.broadcasted_iota(jnp.int32, (8, NB), 0)
+    packed = sums[:, 0:NB]
+    for i in range(1, BLOCKS):
+        packed = jnp.where(sub == i, sums[:, i * NB:(i + 1) * NB], packed)
+    for u in range(NC * PLANE):
+        out_ref[u * UNIT + DATA:(u + 1) * UNIT, :] = packed
+
+
+def gram(pair_scale, row_scale, here, partners, live, descriptors):
+    return pl.pallas_call(
+        lambda *refs: gram_kernel(pair_scale, row_scale, *refs),
+        out_shape=jax.ShapeDtypeStruct((NC * HALF, NB), F32),
+        in_specs=[pl.BlockSpec(memory_space=pltpu.VMEM)] * 4,
+        out_specs=pl.BlockSpec(memory_space=pltpu.VMEM),
+        scratch_shapes=[pltpu.VMEM(here.shape, jnp.bfloat16), pltpu.VMEM((N, N), F32)],
+        compiler_params=pltpu.CompilerParams(vmem_limit_bytes=48 << 20),
+    )(here, partners, live, descriptors)
+
+
+def reduce_kernel(p_ref, out_ref, half, r0, r1, zb, r2, gz, s0, q0, s1, q1, s2, q2, s3, q3, s4, q4, s5, q5):
+    dp, y = lax.axis_index("dp"), lax.axis_index("mp")
+    core, z, x = dp % NC, (dp // NC) % NZ, dp // (NC * NZ)
+    sibling = (dp + 1 - 2 * core, y)
+    mine = x * NY + y
+
+    def plane(o):
+        return (x + o // NY) % NX, (y + o % NY) % NY
+
+    def plane_from(o):
+        return (x + NX - o // NY) % NX, (y + NY - o % NY) % NY
+
+    def plane_id(o):
+        tx, ty = plane(o)
+        return ((tx * NZ + z) * NC + core, ty)
+
+    def line_id(o):
+        return ((x * NZ + (z + o) % NZ) * NC + core, y)
+
+    def rows(base, count):
+        return pl.ds(pl.multiple_of(base, 8), count)
+
+    def send(src, dst, ssem, rsem, target):
+        return pltpu.make_async_remote_copy(
+            src_ref=src, dst_ref=dst, send_sem=ssem, recv_sem=rsem,
+            device_id=target, device_id_type=pl.DeviceIdType.MESH,
+        )
+
+    barrier = pltpu.get_barrier_semaphore()
+    pl.semaphore_signal(barrier, inc=1, device_id=sibling, device_id_type=pl.DeviceIdType.MESH)
+
+    @pl.loop(1, PLANE)
+    def _(o):
+        pl.semaphore_signal(barrier, inc=1, device_id=plane_id(o), device_id_type=pl.DeviceIdType.MESH)
+
+    @pl.loop(1, NZ)
+    def _(o):
+        pl.semaphore_signal(barrier, inc=1, device_id=line_id(o), device_id_type=pl.DeviceIdType.MESH)
+
+    pl.semaphore_wait(barrier, 1 + (PLANE - 1) + (NZ - 1))
+
+    def unit_at(o):
+        tx, ty = plane(o)
+        return (tx * NY + ty) * UNIT
+
+    def copy0(o):
+        at = unit_at(o)
+        return send(p_ref.at[rows((1 - core) * HALF + at, UNIT)], r0.at[rows(at, UNIT)], s0.at[o], q0.at[o], sibling)
+
+    def copy1(o):
+        return send(half.at[rows(unit_at(o), UNIT)], r1.at[o], s1.at[o], q1.at[o], plane_id(o))
+
+    @pl.loop(0, PLANE)
+    def _(i):
+        copy0((i + 1) % PLANE).start()
+
+    zb[UNIT:, :] = jnp.zeros((zb.shape[0] - UNIT, NB), F32)
+
+    @pl.loop(1, PLANE)
+    def _(o):
+        copy0(o).wait_recv()
+        at = unit_at(o)
+        half[rows(at, UNIT), :] = p_ref[rows(core * HALF + at, UNIT), :] + r0[rows(at, UNIT), :]
+        copy1(o).start()
+
+    copy0(0).wait_recv()
+    at = mine * UNIT
+    zb[0:UNIT, :] = p_ref[rows(core * HALF + at, UNIT), :] + r0[rows(at, UNIT), :]
+
+    @pl.loop(1, PLANE)
+    def _(o):
+        copy1(o).wait_recv()
+        zb[0:UNIT, :] = zb[0:UNIT, :] + r1[o]
+
+    def copy2(o):
+        return send(zb.at[rows(((z + o) % NZ) * PIECE, PIECE)], r2.at[o], s2.at[o], q2.at[o], line_id(o))
+
+    def copy3(o, owner):
+        piece = gz.at[rows(owner * PIECE, PIECE)]
+        return send(piece, piece, s3.at[o], q3.at[o], line_id(o))
+
+    @pl.loop(1, NZ)
+    def _(o):
+        copy2(o).start()
+
+    own = rows(z * PIECE, PIECE)
+    gz[own, :] = zb[own, :]
+
+    @pl.loop(1, NZ)
+    def _(o):
+        copy2(o).wait_recv()
+        gz[own, :] = gz[own, :] + r2[o]
+
+    @pl.loop(1, NZ)
+    def _(o):
+        copy3(o, z).start()
+
+    @pl.loop(1, NZ)
+    def _(o):
+        copy3(o, (z + NZ - o) % NZ).wait_recv()
+
+    def copy4(o, unit):
+        return send(gz.at[pl.ds(0, UNIT)], out_ref.at[rows(core * HALF + unit * UNIT, UNIT)], s4.at[o], q4.at[o], plane_id(o))
+
+    def copy5(o, which):
+        tx, ty = plane_from(o)
+        piece = out_ref.at[rows(which * HALF + (tx * NY + ty) * UNIT, UNIT)]
+        return send(piece, piece, s5.at[o], q5.at[o], sibling)
+
+    @pl.loop(1, PLANE)
+    def _(o):
+        copy4(o, mine).start()
+
+    out_ref[rows(core * HALF + mine * UNIT, UNIT), :] = gz[0:UNIT, :]
+    copy5(0, core).start()
+
+    @pl.loop(1, PLANE)
+    def _(o):
+        tx, ty = plane_from(o)
+        copy4(o, tx * NY + ty).wait_recv()
+        copy5(o, core).start()
+
+    @pl.loop(0, PLANE)
+    def _(o):
+        copy5(o, 1 - core).wait_recv()
+        copy5(o, core).wait_send()
+        copy0(o).wait_send()
+
+    @pl.loop(1, PLANE)
+    def _(o):
+        copy1(o).wait_send()
+        copy4(o, mine).wait_send()
+
+    @pl.loop(1, NZ)
+    def _(o):
+        copy2(o).wait_send()
+        copy3(o, z).wait_send()
+
+
+def reduce_all(packed):
+    dma = pltpu.SemaphoreType.DMA
+    return pl.pallas_call(
+        reduce_kernel,
+        out_shape=jax.ShapeDtypeStruct((NC * HALF, NB), F32),
+        in_specs=[pl.BlockSpec(memory_space=pltpu.VMEM)],
+        out_specs=pl.BlockSpec(memory_space=pltpu.VMEM),
+        scratch_shapes=[
+            pltpu.VMEM((HALF, NB), F32),
+            pltpu.VMEM((HALF, NB), F32),
+            pltpu.VMEM((PLANE, UNIT, NB), F32),
+            pltpu.VMEM((NZ * PIECE, NB), F32),
+            pltpu.VMEM((NZ, PIECE, NB), F32),
+            pltpu.VMEM((NZ * PIECE, NB), F32),
+        ] + [dma((PLANE,))] * 4 + [dma((NZ,))] * 4 + [dma((PLANE,))] * 4,
+        compiler_params=pltpu.CompilerParams(
+            collective_id=1, has_side_effects=True, vmem_limit_bytes=40 << 20
+        ),
+    )(packed)
+
+
+def chol_kernel(p_ref, out_ref, mean_ref, c_ref, t_ref):
+    rows_all = R_ALL
+    c_ref[...] = jnp.zeros((N, N), F32)
+    mean_ref[...] = jnp.zeros((8, N), F32)
+    means = p_ref[DATA:UNIT, :] * (1.0 / rows_all)
+    for i in range(BLOCKS):
+        mean_ref[0:1, i * NB:(i + 1) * NB] = means[i:i + 1, :]
+    for i, j, s, at in segments():
+        c_ref[i * NB + s:i * NB + s + SEG, j * NB:(j + 1) * NB] = p_ref[at:at + SEG, :]
     row = lax.broadcasted_iota(jnp.int32, (NB, NB), 0)
     col = lax.broadcasted_iota(jnp.int32, (NB, NB), 1)
+    for i in range(BLOCKS):
+        a = i * NB
+        outer = lax.dot_general(mean_ref[:, a:a + NB], mean_ref[:, a:], contract_rows,
+                                precision=HI, preferred_element_type=F32)
+        c_ref[a:a + NB, a:] = c_ref[a:a + NB, a:] - shrink_weight * outer
+        c_ref[a:a + NB, a:a + NB] = c_ref[a:a + NB, a:a + NB] + jnp.where(row == col, ridge_term, 0.0)
+    blocks = BLOCKS
 
     def step(k, _):
         off = pl.multiple_of(k * NB, NB)
@@ -103,15 +333,15 @@
         out_ref[i * NB:(i + 1) * NB, :] = jnp.where(r >= c, c_ref[i * NB:(i + 1) * NB, :], 0.0).astype(out_ref.dtype)
 
 
-def inverse_factor(metric):
+def inverse_factor(packed):
     return pl.pallas_call(
         chol_kernel,
-        out_shape=jax.ShapeDtypeStruct((N, N), jnp.bfloat16),
+        out_shape=[jax.ShapeDtypeStruct((N, N), jnp.bfloat16), jax.ShapeDtypeStruct((8, N), F32)],
         in_specs=[pl.BlockSpec(memory_space=pltpu.VMEM)],
-        out_specs=pl.BlockSpec(memory_space=pltpu.VMEM),
+        out_specs=[pl.BlockSpec(memory_space=pltpu.VMEM)] * 2,
         scratch_shapes=[pltpu.VMEM((N, N), F32), pltpu.VMEM((NB, NB), F32)],
         compiler_params=pltpu.CompilerParams(vmem_limit_bytes=40 << 20),
-    )(metric)
+    )(packed)
 
 
 def whiten_kernel(db_ref, mean_ref, inv_ref, out_ref):
@@ -137,7 +367,7 @@
         ],
         out_specs=pl.BlockSpec((tile, width), lambda i: (i, 0)),
         compiler_params=pltpu.CompilerParams(vmem_limit_bytes=40 << 20),
-    )(database, jnp.broadcast_to(col_mean[None, :], (8, width)), inverse)
+    )(database, col_mean, inverse)
 
 
 def shards(descriptors, database, anchor_row, partner_row, block_counts):
@@ -158,22 +388,19 @@
     anchors_here = lax.all_to_all(anchors, "dp", split_axis=0, concat_axis=0, tiled=True)
     partners = descriptors.at[jnp.maximum(wanted_here, 0).reshape(-1)].get(
         mode="promise_in_bounds"
-    ).reshape(peer_count, slot_count, feature_width)
-    differences = jnp.where(
-        wanted_here[:, :, None] >= 0, anchors_here.astype(F32) - partners.astype(F32), 0.0
-    )
-    pair_flat = differences.astype(jnp.bfloat16).reshape(-1, feature_width)
-    col_sum = jnp.sum(descriptors, axis=0, dtype=F32)
-    pair_gram = lax.dot_general(pair_flat, pair_flat, contract_rows, preferred_element_type=F32)
-    row_gram = lax.dot_general(
-        descriptors, descriptors, contract_rows, preferred_element_type=F32
-    )
-    partial_sum = pair_gram * (1.0 / pairs_all) + row_gram * (shrink_weight / rows_all)
-    summed, col_total = lax.psum((partial_sum, col_sum), ("dp", "mp"))
-    col_mean = col_total / rows_all
-    identity = jnp.eye(feature_width, dtype=F32)
-    metric = summed - shrink_weight * col_mean[:, None] * col_mean[None, :] + ridge_term * identity
-    return whiten(database, col_mean, inverse_factor(metric))
+    )
+    slots = peer_count * slot_count
+    live = jnp.broadcast_to((wanted_here.reshape(slots, 1) >= 0).astype(F32), (slots, NB))
+    packed = gram(
+        1.0 / pairs_all,
+        shrink_weight / rows_all,
+        anchors_here.reshape(slots, feature_width),
+        partners,
+        live,
+        descriptors,
+    )
+    inverse, col_mean = inverse_factor(reduce_all(packed))
+    return whiten(database, col_mean, inverse)
 
 
 def solution(mesh):

time: 484 us -> 253 us (0.52)
  waiting for transfers between devices: 254 us -> 67.2 us
  blocking collectives: 77 us -> 0 us
  Pallas kernels: 78.7 us -> 143 us
  matrix products: 13.4 us -> 0 us
  between operations: 13.5 us -> 0.12 us
    psum x1 -> x0, waiting for transfers between devices: 187 us -> none  [shards(): summed, col_total = lax.psum((partial_sum, col_sum), ('dp', 'mp'))]
    psum x1 -> x0, blocking collectives: 77 us -> none  [shards(): summed, col_total = lax.psum((partial_sum, col_sum), ('dp', 'mp'))]
    pallas_call x1 -> x3, Pallas kernels: 71 us -> 135 us  [the longest x1 73.1 us: inverse_factor(): pl.pallas_call(chol_kernel, out_shape=[jax.ShapeDtypeStruct((N, N), jnp.b...]
    dot_general x2 -> x0, matrix products: 13.4 us -> none  [the longest x1 8.97 us: shards(): lax.dot_general(pair_flat, pair_flat, contract_rows, preferred_element_ty...]
  transfers between devices with their start and end apart: 3 -> 2, of which waited for: 2 -> 1; matrix products, arithmetic and copies ran while one was open for 4% -> 7% of each run, Pallas kernels for 0% -> 0%
where the time goes in v2:
time: 253 us
  Pallas kernels  143 us (57%)
  waiting for transfers between devices  67.2 us (27%)
  starting transfers between devices  23.6 us (9%)
  local copies, waits for them, and re-layouts  17.6 us (7%)
    pallas_call x1, Pallas kernels, inverse_factor(): pl.pallas_call(chol_kernel, out_shape=[jax.ShapeDtypeStruct((N, N), jnp.b...  73.1 us
    all_to_all x1, waiting for transfers between devices, shards(): lax.all_to_all(anchors, 'dp', split_axis=0, concat_axis=0, tiled=True)  67.2 us
    pallas_call x1, Pallas kernels, reduce_all(): pl.pallas_call(reduce_kernel, out_shape=jax.ShapeDtypeStruct((NC * HALF,...  54.6 us
    all_to_all x1, starting transfers between devices, shards(): lax.all_to_all(wanted, 'dp', split_axis=0, concat_axis=0, tiled=True)  13 us
    all_to_all x1, starting transfers between devices, shards(): lax.all_to_all(anchors, 'dp', split_axis=0, concat_axis=0, tiled=True)  10.6 us
    gather x1, local copies, waits for them, and re-layouts, shards(): descriptors.at[anchor_row[0].reshape(-1)].get(mode='promise_in_bounds')  9.64 us
    pallas_call x1, Pallas kernels, whiten(): pl.pallas_call(whiten_kernel, grid=(rows // tile,), out_shape=jax.ShapeDt...  7.66 us
    pallas_call x1, Pallas kernels, gram(): pl.pallas_call(lambda *refs: gram_kernel(pair_scale, row_scale, *refs), o...  7.63 us
  transfers between devices with their start and end apart: 2, of which 1 were waited for; matrix products, arithmetic and copies ran while one was open for 7% of the time, Pallas kernels for 0%

profile of v2, /device:TPU:1, one launch (start us, length us, event | category | flops | bytes accessed | tf_op | source)
XLA Modules:
  0.0 253.1 jit_solution(2109329962828397987)
XLA Ops:
  0.0 0.8 copy.10
  0.8 1.4 compare_select_fusion
  2.2 13.0 %all-to-all-start.1 = ((s32[64,1,24]{2,1,0:T(1,128)}), s32[64,1,24]{2,1,0:T(1,128)S(1)}, u32[]{:S(2)}, u32[]{:S(2)}) async-start(s32[64,1,24]{2,1,0:T(1,128)} %compare_select_fusion), calls=%async_computation.1 | async-start | bytes 65536 | tf_op jit(solution)/shard_map/all_to_all | solution.py:387
  15.2 0.8 copy.9
  16.0 0.1 reshape_squeeze.3
  16.1 9.6 %gather_fusion = bf16[1536,1024]{1,0:T(8,128)(2,1)} fusion(bf16[1024,1024]{1,0:T(8,128)(2,1)} %refs_3_.1, s32[2048]{0:T(1024)S(1)} %pad_clamp_fusion.1), kind=kCustom, calls=%fused_computation | custom fusion | bytes 6297600 | tf_op jit(solution)/shard_map/gather | solution.py:384
  25.7 0.0 all-to-all-done.1
  25.7 0.0 copy-start
  25.7 10.6 %all-to-all-start = ((bf16[64,24,1024]{2,1,0:T(8,128)(2,1)}), bf16[64,24,1024]{2,1,0:T(8,128)(2,1)}, u32[]{:S(2)}, u32[]{:S(2)}) async-start(bf16[64,24,1024]{2,1,0:T(8,128)(2,1)} %bitcast.4), calls=%async_computation | async-start | bytes 6291456 | tf_op jit(solution)/shard_map/all_to_all | solution.py:388
  36.4 0.1 maximum_reduce_fusion
  36.5 0.1 reshape.124
  36.6 0.0 copy-done
  36.6 5.8 %gather_fusion.1 = bf16[1536,1024]{1,0:T(8,128)(2,1)} fusion(bf16[1024,1024]{1,0:T(8,128)(2,1)S(1)} %copy-done, s32[2048]{0:T(1024)S(1)} %pad_clamp_fusion), kind=kCustom, calls=%fused_computation.1 | custom fusion | bytes 6297600 | tf_op jit(solution)/shard_map/gather | solution.py:389
  42.4 0.1 fusion
  42.5 0.1 reshape.113
  42.6 67.2 %all-to-all-done = bf16[64,24,1024]{2,1,0:T(8,128)(2,1)} async-done(((bf16[64,24,1024]{2,1,0:T(8,128)(2,1)}), bf16[64,24,1024]{2,1,0:T(8,128)(2,1)}, u32[]{:S(2)}, u32[]{:S(2)}) %all-to-all-start) | async-done | bytes 3145760 | tf_op jit(solution)/shard_map/all_to_all | solution.py:388
  109.8 0.3 broadcast_in_dim.12.refs_2_
  110.1 7.6 %shard_map.55.p_ref = f32[4864,128]{1,0:T(8,128)S(1)} custom-call(bf16[1536,1024]{1,0:T(8,128)(2,1)} %bitcast.1.refs_0_, bf16[1536,1024]{1,0:T(8,128)(2,1)} %gather_fusion.1, f32[1536,128]{1,0:T(8,128)S(1)} %broadcast_in_dim.12.refs_2_, bf16[1024,1024]{1,0:T(8,128)(2,1)S(1)} %copy-done), custom_call_target="tpu_custom_call" | custom-call | tf_op jit(solution)/shard_map/pallas_call | solution.py:118
  117.7 0.0 copy-start.1
  117.7 54.6 %shard_map.56.p_ref = f32[4864,128]{1,0:T(8,128)S(1)} custom-call(f32[4864,128]{1,0:T(8,128)S(1)} %shard_map.55.p_ref), custom_call_target="tpu_custom_call" | custom-call | tf_op jit(solution)/shard_map/pallas_call | solution.py:269
  172.3 73.1 %shard_map.57 = (bf16[1024,1024]{1,0:T(8,128)(2,1)S(1)}, f32[8,1024]{1,0:T(8,128)S(1)}) custom-call(f32[4864,128]{1,0:T(8,128)S(1)} %shard_map.56.p_ref), custom_call_target="tpu_custom_call" | custom-call | tf_op jit(solution)/shard_map/pallas_call | solution.py:337
  245.4 0.0 copy-done.1
  245.4 7.7 %shard_map.58 = bf16[2048,1024]{1,0:T(8,128)(2,1)} custom-call(bf16[2048,1024]{1,0:T(8,128)(2,1)S(1)} %copy-done.1, f32[8,1024]{1,0:T(8,128)S(1)} %get-tuple-element.7.mean_ref, bf16[1024,1024]{1,0:T(8,128)(2,1)S(1)} %get-tuple-element.8.inv_ref), custom_call_target="tpu_custom_call" | custom-call | tf_op jit(solution)/shard_map/pallas_call | solution.py:359
  (3 shorter events, 0.0 us)
Async XLA Ops:
  2.2 23.6 %all-to-all-start.1 = ((s32[64,1,24]{2,1,0:T(1,128)}), s32[64,1,24]{2,1,0:T(1,128)S(1)}, u32[]{:S(2)}, u32[]{:S(2)}) async-start(s32[64,1,24]{2,1,0:T(1,128)} %compare_select_fusion), calls=%async_computation.1 | async-start | bytes 65536 | tf_op jit(solution)/shard_map/all_to_all | solution.py:387
  25.7 10.8 %copy-start = (bf16[1024,1024]{1,0:T(8,128)(2,1)S(1)}, bf16[1024,1024]{1,0:T(8,128)(2,1)}, u32[]{:S(2)}) copy-start(bf16[1024,1024]{1,0:T(8,128)(2,1)} %refs_3_.1) | copy-start | bytes 6291460
  25.7 84.1 %all-to-all-start = ((bf16[64,24,1024]{2,1,0:T(8,128)(2,1)}), bf16[64,24,1024]{2,1,0:T(8,128)(2,1)}, u32[]{:S(2)}, u32[]{:S(2)}) async-start(bf16[64,24,1024]{2,1,0:T(8,128)(2,1)} %bitcast.4), calls=%async_computation | async-start | bytes 6291456 | tf_op jit(solution)/shard_map/all_to_all | solution.py:388
  117.7 127.7 %copy-start.1 = (bf16[2048,1024]{1,0:T(8,128)(2,1)S(1)}, bf16[2048,1024]{1,0:T(8,128)(2,1)}, u32[]{:S(2)}) copy-start(bf16[2048,1024]{1,0:T(8,128)(2,1)} %db_ref.1) | copy-start | bytes 12582916

commit v3 on v2

--- a/solution.py
+++ b/solution.py
@@ -1,3 +1,5 @@
+import functools
+
 import jax
 import jax.numpy as jnp
 from jax import lax
@@ -91,19 +93,88 @@
     return found
 
 
-def gram_kernel(pair_scale, row_scale, here_ref, part_ref, live_ref, desc_ref, out_ref, diff_ref, gram_ref):
-    slots = here_ref.shape[0]
+MESH = pl.DeviceIdType.MESH
+CAP = 24
+GROUP = NZ * NC
+PEERS = NX * GROUP
+
+
+def one_hot_rows(index, count):
+    lane = lax.broadcasted_iota(jnp.int32, (count, NB), 1).astype(F32)
+    parts = [jnp.where(index == lane + float(NB * c), 1.0, 0.0).astype(jnp.bfloat16) for c in range(N // NB)]
+    return jnp.concatenate(parts, axis=1)
+
+
+def pairs_kernel(pair_scale, row_scale, anchor_ref, wanted_ref, desc_ref, out_ref,
+                 sbuf, rbuf, windex, wcol, part_ref, diff_ref, gram_ref, s0, q0, s1, q1):
+    dp, y = lax.axis_index("dp"), lax.axis_index("mp")
+    core, z, x = dp % NC, (dp // NC) % NZ, dp // (NC * NZ)
+
+    def peer(ox, o):
+        return ((x + ox) % NX) * GROUP + ((z + o // NC) % NZ) * NC + (core + o % NC) % NC
+
+    def peer_from(ox, o):
+        return ((x + NX - ox) % NX) * GROUP + ((z + NZ - o // NC) % NZ) * NC + (core + NC - o % NC) % NC
+
+    def copy_rows(slot, target, owner):
+        return pltpu.make_async_remote_copy(
+            src_ref=sbuf.at[target], dst_ref=rbuf.at[owner], send_sem=s0.at[slot], recv_sem=q0.at[slot],
+            device_id=(target, y), device_id_type=MESH,
+        )
+
+    def copy_index(slot, target, owner):
+        return pltpu.make_async_remote_copy(
+            src_ref=wanted_ref.at[target], dst_ref=windex.at[owner], send_sem=s1.at[slot], recv_sem=q1.at[slot],
+            device_id=(target, y), device_id_type=MESH,
+        )
+
+    barrier = pltpu.get_barrier_semaphore()
+
+    @pl.loop(1, PEERS)
+    def _(k):
+        pl.semaphore_signal(barrier, inc=1, device_id=(peer(k // GROUP, k % GROUP), y), device_id_type=MESH)
+
+    rows_x = GROUP * CAP
+
+    def gather(ox):
+        group = (x + ox) % NX
+        base = group * rows_x
+        for h in range(2):
+            count = rows_x // 2
+            index = anchor_ref[pl.ds(pl.multiple_of(base + h * count, count), count), :]
+            found = jnp.dot(one_hot_rows(index, count), desc_ref[...], preferred_element_type=F32)
+            for p in range(GROUP // 2):
+                block = found[p * CAP:(p + 1) * CAP, :]
+                block = jnp.concatenate([block[:, :N // 2], block[:, N // 2:]], axis=0)
+                sbuf[group * GROUP + h * (GROUP // 2) + p] = block.astype(jnp.bfloat16)
+
+    gather(0)
+    pl.semaphore_wait(barrier, PEERS - 1)
+
+    @pl.loop(0, NX)
+    def _(ox):
+        @pl.loop(0, GROUP)
+        def _(o):
+            slot = ox * GROUP + o
+
+            @pl.when(slot > 0)
+            def _():
+                copy_rows(slot, peer(ox, o), dp).start()
+
+        @pl.when(ox == 0)
+        def _():
+            @pl.loop(1, PEERS)
+            def _(k):
+                copy_index(k, peer(k // GROUP, k % GROUP), dp).start()
+
+        @pl.when(ox < NX - 1)
+        def _():
+            gather(ox + 1)
+
     tile = 256
-    for r in range(0, slots, tile):
-        gap = here_ref[r:r + tile, :].astype(F32) - part_ref[r:r + tile, :].astype(F32)
-        keep = jnp.broadcast_to(live_ref[r:r + tile, 0:1], gap.shape)
-        diff_ref[r:r + tile, :] = jnp.where(keep > 0.5, gap, 0.0).astype(jnp.bfloat16)
     for i in range(0, N, tile):
-        pair = lax.dot_general(diff_ref[:, i:i + tile], diff_ref[:, i:], contract_rows, preferred_element_type=F32)
-        row = lax.dot_general(desc_ref[:, i:i + tile], desc_ref[:, i:], contract_rows, preferred_element_type=F32)
-        gram_ref[i:i + tile, i:] = pair * pair_scale + row * row_scale
-    for i, j, s, at in segments():
-        out_ref[at:at + SEG, :] = gram_ref[i * NB + s:i * NB + s + SEG, j * NB:(j + 1) * NB]
+        gram_ref[i:i + tile, i:] = row_scale * lax.dot_general(
+            desc_ref[:, i:i + tile], desc_ref[:, i:], contract_rows, preferred_element_type=F32)
     ones = jnp.ones((8, desc_ref.shape[0]), jnp.bfloat16)
     sums = jnp.dot(ones, desc_ref[...], preferred_element_type=F32)
     sub = lax.broadcasted_iota(jnp.int32, (8, NB), 0)
@@ -113,16 +184,83 @@
     for u in range(NC * PLANE):
         out_ref[u * UNIT + DATA:(u + 1) * UNIT, :] = packed
 
-
-def gram(pair_scale, row_scale, here, partners, live, descriptors):
+    windex[dp] = wanted_ref[dp]
+
+    @pl.loop(1, PEERS)
+    def _(k):
+        copy_index(k, peer(k // GROUP, k % GROUP), peer_from(k // GROUP, k % GROUP)).wait_recv()
+
+    turned = windex[...].reshape(PEERS, NB)
+    turned = jnp.concatenate([turned, jnp.zeros((NB - PEERS, NB), F32)], axis=0).T
+    for p in range(PEERS):
+        wcol[p * CAP:(p + 1) * CAP, :] = jnp.broadcast_to(turned[0:CAP, p:p + 1], (CAP, NB))
+
+    count = 192
+
+    @pl.loop(0, PEERS * CAP // count)
+    def _(g):
+        at = pl.ds(pl.multiple_of(g * count, count), count)
+        found = jnp.dot(one_hot_rows(wcol[at, :], count), desc_ref[...], preferred_element_type=F32)
+        part_ref[at, :] = found.astype(jnp.bfloat16)
+
+    rbuf[dp] = sbuf[dp]
+
+    @pl.loop(0, NX)
+    def _(ox):
+        group = (x + NX - ox) % NX
+
+        @pl.loop(0, GROUP)
+        def _(o):
+            slot = ox * GROUP + o
+
+            @pl.when(slot > 0)
+            def _():
+                copy_rows(slot, peer(ox, o), peer_from(ox, o)).wait_recv()
+
+        @pl.loop(0, GROUP // 2)
+        def _(m):
+            first = group * GROUP + 2 * m
+            blocks = []
+            for e in range(2):
+                got = rbuf[first + e].astype(F32)
+                blocks.append(jnp.concatenate([got[:CAP], got[CAP:]], axis=1))
+            at = pl.multiple_of(first * CAP, 2 * CAP)
+            gap = jnp.concatenate(blocks, axis=0) - part_ref[pl.ds(at, 2 * CAP), :].astype(F32)
+            diff_ref[pl.ds(pl.multiple_of(m * 2 * CAP, 2 * CAP), 2 * CAP), :] = gap.astype(jnp.bfloat16)
+
+        for i in range(0, N, tile):
+            gram_ref[i:i + tile, i:] = gram_ref[i:i + tile, i:] + pair_scale * lax.dot_general(
+                diff_ref[:, i:i + tile], diff_ref[:, i:], contract_rows, preferred_element_type=F32)
+
+    for i, j, s, at in segments():
+        out_ref[at:at + SEG, :] = gram_ref[i * NB + s:i * NB + s + SEG, j * NB:(j + 1) * NB]
+
+    @pl.loop(1, PEERS)
+    def _(k):
+        copy_rows(k, peer(k // GROUP, k % GROUP), dp).wait_send()
+        copy_index(k, peer(k // GROUP, k % GROUP), dp).wait_send()
+
+
+def pair_grams(pair_scale, row_scale, anchor, wanted, descriptors):
+    dma = pltpu.SemaphoreType.DMA
     return pl.pallas_call(
-        lambda *refs: gram_kernel(pair_scale, row_scale, *refs),
+        functools.partial(pairs_kernel, pair_scale, row_scale),
         out_shape=jax.ShapeDtypeStruct((NC * HALF, NB), F32),
-        in_specs=[pl.BlockSpec(memory_space=pltpu.VMEM)] * 4,
+        in_specs=[pl.BlockSpec(memory_space=pltpu.VMEM)] * 3,
         out_specs=pl.BlockSpec(memory_space=pltpu.VMEM),
-        scratch_shapes=[pltpu.VMEM(here.shape, jnp.bfloat16), pltpu.VMEM((N, N), F32)],
-        compiler_params=pltpu.CompilerParams(vmem_limit_bytes=48 << 20),
-    )(here, partners, live, descriptors)
+        scratch_shapes=[
+            pltpu.VMEM((PEERS, 2 * CAP, N // 2), jnp.bfloat16),
+            pltpu.VMEM((PEERS, 2 * CAP, N // 2), jnp.bfloat16),
+            pltpu.VMEM((PEERS, 1, NB), F32),
+            pltpu.VMEM((PEERS * CAP, NB), F32),
+            pltpu.VMEM((PEERS * CAP, N), jnp.bfloat16),
+            pltpu.VMEM((GROUP * CAP, N), jnp.bfloat16),
+            pltpu.VMEM((N, N), F32),
+        ] + [dma((PEERS,))] * 4,
+        compiler_params=pltpu.CompilerParams(
+            collective_id=2, has_side_effects=True, vmem_limit_bytes=48 << 20
+        ),
+    )(anchor, wanted, descriptors)
 
 
 def reduce_kernel(p_ref, out_ref, half, r0, r1, zb, r2, gz, s0, q0, s1, q1, s2, q2, s3, q3, s4, q4, s5, q5):
@@ -371,7 +509,6 @@
 
 
 def shards(descriptors, database, anchor_row, partner_row, block_counts):
-    feature_width = descriptors.shape[1]
     local_rows = descriptors.shape[0]
     peer_count = partner_row.shape[1]
     slot_count = partner_row.shape[2]
@@ -380,23 +517,14 @@
     rows_all = local_rows * devices
     slot_iota = lax.broadcasted_iota(jnp.int32, (peer_count, slot_count), 1)
     live_slots = slot_iota < block_counts[0][:, None]
-    wanted = jnp.where(live_slots, partner_row[0], -1)
-    anchors = descriptors.at[anchor_row[0].reshape(-1)].get(mode="promise_in_bounds").reshape(
-        peer_count, slot_count, feature_width
-    )
-    wanted_here = lax.all_to_all(wanted, "dp", split_axis=0, concat_axis=0, tiled=True)
-    anchors_here = lax.all_to_all(anchors, "dp", split_axis=0, concat_axis=0, tiled=True)
-    partners = descriptors.at[jnp.maximum(wanted_here, 0).reshape(-1)].get(
-        mode="promise_in_bounds"
-    )
-    slots = peer_count * slot_count
-    live = jnp.broadcast_to((wanted_here.reshape(slots, 1) >= 0).astype(F32), (slots, NB))
-    packed = gram(
+    wanted = jnp.where(live_slots, partner_row[0], -1).astype(F32)
+    wanted = jnp.pad(wanted, ((0, 0), (0, NB - slot_count)))[:, None, :]
+    anchor = jnp.where(live_slots, anchor_row[0], -1).astype(F32).reshape(-1, 1)
+    packed = pair_grams(
         1.0 / pairs_all,
         shrink_weight / rows_all,
-        anchors_here.reshape(slots, feature_width),
-        partners,
-        live,
+        jnp.broadcast_to(anchor, (peer_count * slot_count, NB)),
+        wanted,
         descriptors,
     )
     inverse, col_mean = inverse_factor(reduce_all(packed))

time: 253 us -> 232 us (0.917)
  Pallas kernels: 143 us -> 227 us
  waiting for transfers between devices: 67.2 us -> 0 us
  starting transfers between devices: 23.6 us -> 0 us
  local copies, waits for them, and re-layouts: 17.6 us -> 3.62 us
    pallas_call x1, Pallas kernels: 7.63 us -> 88.5 us  [pair_grams(): pl.pallas_call(functools.partial(pairs_kernel, pair_scale, row_scale), ou...]
    all_to_all x2 -> x0, waiting for transfers between devices: 67.2 us -> none  [the longest x1 67.2 us: shards(): lax.all_to_all(anchors, 'dp', split_axis=0, concat_axis=0, tiled=True)]
    all_to_all x2 -> x0, starting transfers between devices: 23.6 us -> none  [the longest x1 13 us: shards(): lax.all_to_all(wanted, 'dp', split_axis=0, concat_axis=0, tiled=True)]
    gather x2 -> x0, local copies, waits for them, and re-layouts: 15.5 us -> none  [the longest x1 9.64 us: shards(): descriptors.at[anchor_row[0].reshape(-1)].get(mode='promise_in_bounds')]
    pallas_call x1, Pallas kernels: 54.6 us -> 58 us  [reduce_all(): pl.pallas_call(reduce_kernel, out_shape=jax.ShapeDtypeStruct((NC * HALF,...]
  transfers between devices with their start and end apart: 2 -> 0, of which waited for: 1 -> 0; matrix products, arithmetic and copies ran while one was open for 7% -> 0% of each run, Pallas kernels for 0% -> 0%
where the time goes in v3:
time: 232 us
  Pallas kernels  227 us (98%)
  local copies, waits for them, and re-layouts  3.62 us (2%)
    pallas_call x1, Pallas kernels, pair_grams(): pl.pallas_call(functools.partial(pairs_kernel, pair_scale, row_scale), ou...  88.5 us
    pallas_call x1, Pallas kernels, inverse_factor(): pl.pallas_call(chol_kernel, out_shape=[jax.ShapeDtypeStruct((N, N), jnp.b...  72.9 us
    pallas_call x1, Pallas kernels, reduce_all(): pl.pallas_call(reduce_kernel, out_shape=jax.ShapeDtypeStruct((NC * HALF,...  58 us
    pallas_call x1, Pallas kernels, whiten(): pl.pallas_call(whiten_kernel, grid=(rows // tile,), out_shape=jax.ShapeDt...  7.66 us

profile of v3, /device:TPU:1, one launch (start us, length us, event | category | flops | bytes accessed | tf_op | source)
XLA Modules:
  0.0 232.2 jit_solution(12375735164968243550)
XLA Ops:
  0.0 0.7 iota_compare_fusion
  0.7 0.1 lt.20
  0.8 0.8 copy.7
  1.6 0.1 squeeze.6
  1.7 0.8 copy.8
  2.5 0.7 fusion
  3.3 0.3 broadcast_in_dim.16.anchor_ref
  3.5 0.0 copy-start.1
  3.5 1.6 copy-done.1
  5.1 88.5 %shard_map.55.p_ref = f32[4864,128]{1,0:T(8,128)S(1)} custom-call(f32[1536,128]{1,0:T(8,128)S(1)} %broadcast_in_dim.16.anchor_ref, f32[64,1,128]{2,1,0:T(1,128)S(1)} %bitcast.6, bf16[1024,1024]{1,0:T(8,128)(2,1)S(1)} %copy-done.1), custom_call_target="tpu_custom_call" | custom-call | tf_op jit(solution)/shard_map/pallas_call | solution.py:246
  93.6 0.0 copy-start
  93.6 58.0 %shard_map.56.p_ref = f32[4864,128]{1,0:T(8,128)S(1)} custom-call(f32[4864,128]{1,0:T(8,128)S(1)} %shard_map.55.p_ref), custom_call_target="tpu_custom_call" | custom-call | tf_op jit(solution)/shard_map/pallas_call | solution.py:407
  151.6 72.9 %shard_map.57 = (bf16[1024,1024]{1,0:T(8,128)(2,1)S(1)}, f32[8,1024]{1,0:T(8,128)S(1)}) custom-call(f32[4864,128]{1,0:T(8,128)S(1)} %shard_map.56.p_ref), custom_call_target="tpu_custom_call" | custom-call | tf_op jit(solution)/shard_map/pallas_call | solution.py:475
  224.6 0.0 copy-done
  224.6 7.7 %shard_map.58 = bf16[2048,1024]{1,0:T(8,128)(2,1)} custom-call(bf16[2048,1024]{1,0:T(8,128)(2,1)S(1)} %copy-done, f32[8,1024]{1,0:T(8,128)S(1)} %get-tuple-element.7.mean_ref, bf16[1024,1024]{1,0:T(8,128)(2,1)S(1)} %get-tuple-element.8.inv_ref), custom_call_target="tpu_custom_call" | custom-call | tf_op jit(solution)/shard_map/pallas_call | solution.py:497
  (2 shorter events, 0.0 us)
Async XLA Ops:
  3.5 1.6 copy-start.1
  93.6 131.0 %copy-start = (bf16[2048,1024]{1,0:T(8,128)(2,1)S(1)}, bf16[2048,1024]{1,0:T(8,128)(2,1)}, u32[]{:S(2)}) copy-start(bf16[2048,1024]{1,0:T(8,128)(2,1)} %db_ref.1) | copy-start | bytes 12582916

commit v4 on v1

v4 whole, which is shorter than its diff:
```python
import functools

import jax
import jax.numpy as jnp
from jax import lax
from jax.experimental import pallas as pl
from jax.experimental.pallas import tpu as pltpu
from jax.sharding import PartitionSpec as P

PAIRS_DEV = 1024


shrink_weight = 0.5
ridge_term = 0.05
norm_epsilon = 1e-06
contract_rows = (((0,), (0,)), ((), ()))

N = 1024
NB = 128
F32 = jnp.float32
HI = lax.Precision.HIGHEST
MESH = pl.DeviceIdType.MESH

def lane_bcast(x, c):
    return jnp.take_along_axis(x, jnp.full(x.shape, c, jnp.int32), axis=1, mode="promise_in_bounds")


def row_bcast(x, i):
    return jnp.broadcast_to(x[i:i + 1, :], x.shape)


def factor_block(rows):
    lane = lax.broadcasted_iota(jnp.int32, (8, NB), 1)
    sub = lax.broadcasted_iota(jnp.int32, (8, NB), 0)
    count = len(rows)
    for q in range(count):
        base = 8 * q
        inside = (lane >= base) & (lane < base + 8)
        own = [row_bcast(rows[q], i) for i in range(8)]
        d = {}
        for j in range(8):
            for i in range(j, 8):
                d[i, j] = lane_bcast(own[i], base + j)
        w = [jnp.where(inside, jnp.where(lane == base + i, 1.0, 0.0), own[i]) for i in range(8)]
        ahead = q + 1 < count
        v = [lane_bcast(rows[q + 1], base + j) for j in range(8)] if ahead else None
        inv, scale, low = [], [], {}
        for j in range(8):
            s = lax.rsqrt(d[j, j])
            r = s * s
            inv.append(r)
            scale.append(s)
            for i in range(j + 1, 8):
                low[i, j] = d[i, j] * r
            for i in range(j + 1, 8):
                for k in range(j + 1, i + 1):
                    d[i, k] = d[i, k] - low[i, j] * d[k, j]
            for i in range(j + 1, 8):
                w[i] = w[i] - low[i, j] * w[j]
                if ahead:
                    v[i] = v[i] - low[i, j] * v[j]
        if ahead:
            following = jnp.where(inside, 0.0, rows[q + 1])
            for j in range(8):
                following = following - v[j] * (inv[j] * w[j])
        g = [None] * 8
        for i in range(7, -1, -1):
            acc = inv[i] * w[i]
            for j in range(i + 1, 8):
                acc = acc - low[j, i] * g[j]
            g[i] = acc
        out = scale[0] * w[0]
        for i in range(1, 8):
            out = jnp.where(sub == i, scale[i] * w[i], out)
        rows[q] = out
        for t in range(q + 2, count):
            acc = jnp.where(inside, 0.0, rows[t])
            for j in range(8):
                acc = acc - lane_bcast(rows[t], base + j) * g[j]
            rows[t] = acc
        if ahead:
            rows[q + 1] = following
    return rows


NX, NY, NZ, NC = 4, 4, 8, 2
PLANE = NX * NY
BLOCKS = N // NB
CAP = 24
GROUP = NZ * NC
PEERS = NX * GROUP
CUT = N // 2
LEFT = [(i, j) for j in range(BLOCKS // 2) for i in range(j + 1)]
RIGHT = [(i, j) for j in range(BLOCKS // 2, BLOCKS) for i in range(j + 1)]
DATA_LEFT = len(LEFT) * NB // (NC * PLANE)
UNIT_LEFT = DATA_LEFT + 8
UNIT_RIGHT = len(RIGHT) * NB // (NC * PLANE)
PIECE_LEFT, PIECE_RIGHT = 8, 16


def segments(blocks, data, unit):
    found = []
    for b, (i, j) in enumerate(blocks):
        for s in range(0, NB, 8):
            flat = b * NB + s
            found.append((i * NB + s, j * NB, flat // data * unit + flat % data))
    return found


def one_hot_rows(index, count):
    lane = lax.broadcasted_iota(jnp.int32, (count, NB), 1).astype(F32)
    parts = [jnp.where(index == lane + float(NB * c), 1.0, 0.0).astype(jnp.bfloat16) for c in range(N // NB)]
    return jnp.concatenate(parts, axis=1)


def rows_at(base, count):
    return pl.ds(pl.multiple_of(base, 8), count)


class Sum:
    def __init__(self, unit, piece, p_ref, out_ref, half, r0, r1, zb, r2, gz, near, far):
        self.unit, self.piece, self.half_rows = unit, piece, PLANE * unit
        self.p, self.out, self.half, self.r0, self.r1 = p_ref, out_ref, half, r0, r1
        self.zb, self.r2, self.gz, self.near, self.far = zb, r2, gz, near, far
        dp, self.y = lax.axis_index("dp"), lax.axis_index("mp")
        self.core, self.z, self.x = dp % NC, (dp // NC) % NZ, dp // (NC * NZ)
        self.sibling = (dp + 1 - 2 * self.core, self.y)
        self.mine = self.x * NY + self.y

    def plane(self, o):
        return (self.x + o // NY) % NX, (self.y + o % NY) % NY

    def plane_from(self, o):
        return (self.x + NX - o // NY) % NX, (self.y + NY - o % NY) % NY

    def plane_id(self, o):
        tx, ty = self.plane(o)
        return ((tx * NZ + self.z) * NC + self.core, ty)

    def line_id(self, o):
        return ((self.x * NZ + (self.z + o) % NZ) * NC + self.core, self.y)

    def near_copy(self, pair, o, src, dst, target):
        return pltpu.make_async_remote_copy(
            src_ref=src, dst_ref=dst, send_sem=self.near.at[2 * pair, o], recv_sem=self.near.at[2 * pair + 1, o],
            device_id=target, device_id_type=MESH)

    def far_copy(self, pair, o, src, dst, target):
        return pltpu.make_async_remote_copy(
            src_ref=src, dst_ref=dst, send_sem=self.far.at[2 * pair, o], recv_sem=self.far.at[2 * pair + 1, o],
            device_id=target, device_id_type=MESH)

    def unit_at(self, o):
        tx, ty = self.plane(o)
        return (tx * NY + ty) * self.unit

    def copy0(self, o):
        at = self.unit_at(o)
        src = self.p.at[rows_at((1 - self.core) * self.half_rows + at, self.unit)]
        return self.near_copy(0, o, src, self.r0.at[rows_at(at, self.unit)], self.sibling)

    def copy1(self, o):
        return self.near_copy(1, o, self.half.at[rows_at(self.unit_at(o), self.unit)], self.r1.at[o], self.plane_id(o))

    def copy2(self, o):
        src = self.zb.at[rows_at(((self.z + o) % NZ) * self.piece, self.piece)]
        return self.far_copy(0, o, src, self.r2.at[o], self.line_id(o))

    def copy3(self, o, owner):
        part = self.gz.at[rows_at(owner * self.piece, self.piece)]
        return self.far_copy(1, o, part, part, self.line_id(o))

    def copy4(self, o, owner):
        dst = self.out.at[rows_at(self.core * self.half_rows + owner * self.unit, self.unit)]
        return self.near_copy(2, o, self.gz.at[pl.ds(0, self.unit)], dst, self.plane_id(o))

    def copy5(self, o, which):
        tx, ty = self.plane_from(o)
        part = self.out.at[rows_at(which * self.half_rows + (tx * NY + ty) * self.unit, self.unit)]
        return self.near_copy(3, o, part, part, self.sibling)

    def to_sibling(self):
        @pl.loop(0, PLANE)
        def _(i):
            self.copy0((i + 1) % PLANE).start()

        pad = self.zb.shape[0] - self.unit
        self.zb[self.unit:, :] = jnp.zeros((pad, NB), F32)

    def to_plane(self):
        @pl.loop(1, PLANE)
        def _(o):
            self.copy0(o).wait_recv()
            at = self.unit_at(o)
            own = self.p[rows_at(self.core * self.half_rows + at, self.unit), :]
            self.half[rows_at(at, self.unit), :] = own + self.r0[rows_at(at, self.unit), :]
            self.copy1(o).start()

        self.copy0(0).wait_recv()
        at = self.mine * self.unit
        own = self.p[rows_at(self.core * self.half_rows + at, self.unit), :]
        self.zb[0:self.unit, :] = own + self.r0[rows_at(at, self.unit), :]

    def to_line(self):
        @pl.loop(1, PLANE)
        def _(o):
            self.copy1(o).wait_recv()
            self.zb[0:self.unit, :] = self.zb[0:self.unit, :] + self.r1[o]

        @pl.loop(1, NZ)
        def _(o):
            self.copy2(o).start()

        own = rows_at(self.z * self.piece, self.piece)
        self.gz[own, :] = self.zb[own, :]

        @pl.loop(1, NZ)
        def _(o):
            self.copy2(o).wait_recv()
            self.gz[own, :] = self.gz[own, :] + self.r2[o]

        @pl.loop(1, NZ)
        def _(o):
            self.copy3(o, self.z).start()

        @pl.loop(1, NZ)
        def _(o):
            self.copy3(o, (self.z + NZ - o) % NZ).wait_recv()

        @pl.loop(1, PLANE)
        def _(o):
            self.copy4(o, self.mine).start()

        self.out[rows_at(self.core * self.half_rows + self.mine * self.unit, self.unit), :] = self.gz[0:self.unit, :]
        self.copy5(0, self.core).start()

    def finish(self):
        @pl.loop(1, PLANE)
        def _(o):
            tx, ty = self.plane_from(o)
            self.copy4(o, tx * NY + ty).wait_recv()
            self.copy5(o, self.core).start()

        @pl.loop(0, PLANE)
        def _(o):
            self.copy5(o, 1 - self.core).wait_recv()
            self.copy5(o, self.core).wait_send()
            self.copy0(o).wait_send()

        @pl.loop(1, PLANE)
        def _(o):
            self.copy1(o).wait_send()
            self.copy4(o, self.mine).wait_send()

        @pl.loop(1, NZ)
        def _(o):
            self.copy2(o).wait_send()
            self.copy3(o, self.z).wait_send()


def factor_kernel(pair_scale, row_scale, rows_all, anchor_ref, wanted_ref, desc_ref, out_ref, mean_ref,
                  sbuf, rbuf, windex, wcol, part_ref, diff_ref, gram_ref, c_ref, t_ref, s0, q0, s1, q1,
                  *sums):
    dp, y = lax.axis_index("dp"), lax.axis_index("mp")
    core, z, x = dp % NC, (dp // NC) % NZ, dp // (NC * NZ)
    left = Sum(UNIT_LEFT, PIECE_LEFT, *sums[:10])
    right = Sum(UNIT_RIGHT, PIECE_RIGHT, *sums[10:])

    def peer(ox, o):
        return ((x + ox) % NX) * GROUP + ((z + o // NC) % NZ) * NC + (core + o % NC) % NC

    def peer_from(ox, o):
        return ((x + NX - ox) % NX) * GROUP + ((z + NZ - o // NC) % NZ) * NC + (core + NC - o % NC) % NC

    def copy_rows(part, slot, target, owner):
        return pltpu.make_async_remote_copy(
            src_ref=sbuf.at[part, target], dst_ref=rbuf.at[part, owner], send_sem=s0.at[part, slot],
            recv_sem=q0.at[part, slot], device_id=(target, y), device_id_type=MESH)

    def copy_index(slot, target, owner):
        return pltpu.make_async_remote_copy(
            src_ref=wanted_ref.at[target], dst_ref=windex.at[owner], send_sem=s1.at[slot], recv_sem=q1.at[slot],
            device_id=(target, y), device_id_type=MESH)

    barrier = pltpu.get_barrier_semaphore()

    @pl.loop(1, PEERS)
    def _(k):
        pl.semaphore_signal(barrier, inc=1, device_id=(peer(k // GROUP, k % GROUP), y), device_id_type=MESH)

    @pl.loop(1, PLANE)
    def _(o):
        @pl.when(o % NY != 0)
        def _():
            pl.semaphore_signal(barrier, inc=1, device_id=left.plane_id(o), device_id_type=MESH)

    rows_x = GROUP * CAP

    def gather(ox):
        group = (x + ox) % NX
        base = group * rows_x
        for h in range(2):
            count = rows_x // 2
            index = anchor_ref[pl.ds(pl.multiple_of(base + h * count, count), count), :]
            found = jnp.dot(one_hot_rows(index, count), desc_ref[...], preferred_element_type=F32)
            for p in range(GROUP // 2):
                block = found[p * CAP:(p + 1) * CAP, :]
                for part in range(2):
                    a = part * CUT
                    halves = jnp.concatenate([block[:, a:a + CUT // 2], block[:, a + CUT // 2:a + CUT]], axis=0)
                    sbuf[part, group * GROUP + h * (GROUP // 2) + p] = halves.astype(jnp.bfloat16)

    gather(0)
    pl.semaphore_wait(barrier, PEERS - 1 + PLANE - NX)

    @pl.loop(0, NX)
    def _(ox):
        @pl.loop(0, GROUP)
        def _(o):
            slot = ox * GROUP + o

            @pl.when(slot > 0)
            def _():
                copy_rows(0, slot, peer(ox, o), dp).start()

        @pl.when(ox == 0)
        def _():
            @pl.loop(1, PEERS)
            def _(k):
                copy_index(k, peer(k // GROUP, k % GROUP), dp).start()

        @pl.when(ox < NX - 1)
        def _():
            gather(ox + 1)

    @pl.loop(1, PEERS)
    def _(k):
        copy_rows(1, k, peer(k // GROUP, k % GROUP), dp).start()

    tile = 256
    for i in range(0, N, tile):
        gram_ref[i:i + tile, i:] = row_scale * lax.dot_general(
            desc_ref[:, i:i + tile], desc_ref[:, i:], contract_rows, preferred_element_type=F32)
    ones = jnp.ones((8, desc_ref.shape[0]), jnp.bfloat16)
    sums_row = jnp.dot(ones, desc_ref[...], preferred_element_type=F32)
    sub = lax.broadcasted_iota(jnp.int32, (8, NB), 0)
    packed = sums_row[:, 0:NB]
    for i in range(1, BLOCKS):
        packed = jnp.where(sub == i, sums_row[:, i * NB:(i + 1) * NB], packed)
    for u in range(NC * PLANE):
        left.p[u * UNIT_LEFT + DATA_LEFT:(u + 1) * UNIT_LEFT, :] = packed

    windex[dp] = wanted_ref[dp]

    @pl.loop(1, PEERS)
    def _(k):
        copy_index(k, peer(k // GROUP, k % GROUP), peer_from(k // GROUP, k % GROUP)).wait_recv()

    turned = windex[...].reshape(PEERS, NB)
    turned = jnp.concatenate([turned, jnp.zeros((NB - PEERS, NB), F32)], axis=0).T
    for p in range(PEERS):
        wcol[p * CAP:(p + 1) * CAP, :] = jnp.broadcast_to(turned[0:CAP, p:p + 1], (CAP, NB))

    count = 192

    @pl.loop(0, PEERS * CAP // count)
    def _(g):
        at = pl.ds(pl.multiple_of(g * count, count), count)
        found = jnp.dot(one_hot_rows(wcol[at, :], count), desc_ref[...], preferred_element_type=F32)
        part_ref[at, :] = found.astype(jnp.bfloat16)

    rbuf[0, dp] = sbuf[0, dp]
    rbuf[1, dp] = sbuf[1, dp]

    def receive(part):
        a = part * CUT

        @pl.loop(0, NX)
        def _(ox):
            group = (x + NX - ox) % NX
            start = ox * rows_x

            @pl.loop(0, GROUP)
            def _(o):
                slot = ox * GROUP + o

                @pl.when(slot > 0)
                def _():
                    copy_rows(part, slot, peer(ox, o), peer_from(ox, o)).wait_recv()

            @pl.loop(0, GROUP // 2)
            def _(m):
                first = group * GROUP + 2 * m
                blocks = []
                for e in range(2):
                    got = rbuf[part, first + e].astype(F32)
                    blocks.append(jnp.concatenate([got[:CAP], got[CAP:]], axis=1))
                at = pl.multiple_of(first * CAP, 2 * CAP)
                gap = jnp.concatenate(blocks, axis=0) - part_ref[pl.ds(at, 2 * CAP), a:a + CUT].astype(F32)
                to = pl.multiple_of(start + m * 2 * CAP, 2 * CAP)
                diff_ref[pl.ds(to, 2 * CAP), a:a + CUT] = gap.astype(jnp.bfloat16)

            here = pl.ds(pl.multiple_of(start, rows_x), rows_x)
            for i in range(0, a + CUT, tile):
                b = max(i, a)
                gram_ref[i:i + tile, b:a + CUT] = gram_ref[i:i + tile, b:a + CUT] + pair_scale * lax.dot_general(
                    diff_ref[here, i:i + tile], diff_ref[here, b:a + CUT], contract_rows, preferred_element_type=F32)

    def metric(first_block, last_block):
        row = lax.broadcasted_iota(jnp.int32, (NB, NB), 0)
        col = lax.broadcasted_iota(jnp.int32, (NB, NB), 1)
        for i in range(last_block):
            a, b, e = i * NB, max(i, first_block) * NB, last_block * NB
            outer = lax.dot_general(mean_ref[:, a:a + NB], mean_ref[:, b:e], contract_rows,
                                    precision=HI, preferred_element_type=F32)
            c_ref[a:a + NB, b:e] = c_ref[a:a + NB, b:e] - shrink_weight * outer
            if i >= first_block:
                c_ref[a:a + NB, a:a + NB] = c_ref[a:a + NB, a:a + NB] + jnp.where(row == col, ridge_term, 0.0)

    receive(0)
    for r, c, at in segments(LEFT, DATA_LEFT, UNIT_LEFT):
        left.p[at:at + 8, :] = gram_ref[r:r + 8, c:c + NB]
    left.to_sibling()
    c_ref[...] = jnp.zeros((N, N), F32)
    mean_ref[...] = jnp.zeros((8, N), F32)
    left.to_plane()
    left.to_line()
    left.finish()
    means = left.out[DATA_LEFT:UNIT_LEFT, :] * (1.0 / rows_all)
    for i in range(BLOCKS):
        mean_ref[0:1, i * NB:(i + 1) * NB] = means[i:i + 1, :]
    for r, c, at in segments(LEFT, DATA_LEFT, UNIT_LEFT):
        c_ref[r:r + 8, c:c + NB] = left.out[at:at + 8, :]
    metric(0, BLOCKS // 2)

    receive(1)
    for r, c, at in segments(RIGHT, UNIT_RIGHT, UNIT_RIGHT):
        right.p[at:at + 8, :] = gram_ref[r:r + 8, c:c + NB]
    right.to_sibling()

    cut_block = BLOCKS // 2
    row = lax.broadcasted_iota(jnp.int32, (NB, NB), 0)
    col = lax.broadcasted_iota(jnp.int32, (NB, NB), 1)

    def step(k, _):
        @pl.when(k == 1)
        def _():
            right.to_plane()

        @pl.when(k == 3)
        def _():
            right.to_line()

        @pl.when(k == cut_block)
        def _():
            right.finish()
            for r, c, at in segments(RIGHT, UNIT_RIGHT, UNIT_RIGHT):
                c_ref[r:r + 8, c:c + NB] = right.out[at:at + 8, :]
            metric(cut_block, BLOCKS)
            r = lax.broadcasted_iota(jnp.int32, (CUT, CUT), 0)
            c = lax.broadcasted_iota(jnp.int32, (CUT, CUT), 1)
            gram_ref[0:CUT, 0:CUT] = jnp.where(r >= c, c_ref[0:CUT, 0:CUT], 0.0)
            upper = jnp.dot(gram_ref[0:CUT, 0:CUT], c_ref[0:CUT, CUT:], precision=HI, preferred_element_type=F32)
            c_ref[0:CUT, CUT:] = upper
            c_ref[CUT:, 0:CUT] = -lax.dot_general(c_ref[0:CUT, CUT:], gram_ref[0:CUT, 0:CUT], contract_rows,
                                                  precision=HI, preferred_element_type=F32)
            c_ref[CUT:, CUT:] = c_ref[CUT:, CUT:] - lax.dot_general(
                c_ref[0:CUT, CUT:], c_ref[0:CUT, CUT:], contract_rows, precision=HI, preferred_element_type=F32)

        off = pl.multiple_of(k * NB, NB)
        diag = c_ref.at[pl.ds(off, NB), pl.ds(off, NB)]
        rows = factor_block([diag[8 * q:8 * q + 8, :] for q in range(NB // 8)])
        for q in range(NB // 8):
            t_ref[8 * q:8 * q + 8, :] = rows[q]
        t = jnp.where(row >= col, t_ref[...], 0.0)

        @pl.when(k < cut_block)
        def _():
            c_ref[pl.ds(off, NB), 0:CUT] = jnp.dot(
                t, c_ref[pl.ds(off, NB), 0:CUT], precision=HI, preferred_element_type=F32)

        @pl.when(k >= cut_block)
        def _():
            c_ref[pl.ds(off, NB), :] = jnp.dot(
                t, c_ref[pl.ds(off, NB), :], precision=HI, preferred_element_type=F32)

        c_ref[pl.ds(off, NB), pl.ds(off, NB)] = t

        for now in range(BLOCKS - 1):
            if now == cut_block - 1:
                continue

            @pl.when(k == now)
            def _(now=now):
                at, nxt = now * NB, (now + 1) * NB
                end = CUT if now < cut_block else N
                u = c_ref[at:nxt, nxt:end]
                prod = lax.dot_general(u, c_ref[at:nxt, 0:nxt], contract_rows, precision=HI,
                                       preferred_element_type=F32)
                if now:
                    c_ref[nxt:end, 0:at] = c_ref[nxt:end, 0:at] - prod[:, 0:at]
                c_ref[nxt:end, at:nxt] = -prod[:, at:nxt]
                for r in range(nxt, end, 2 * NB):
                    h = min(2 * NB, end - r)
                    prod = lax.dot_general(u[:, r - nxt:r - nxt + h], c_ref[at:nxt, r:end], contract_rows,
                                           precision=HI, preferred_element_type=F32)
                    c_ref[r:r + h, r:end] = c_ref[r:r + h, r:end] - prod
        return 0

    lax.fori_loop(0, BLOCKS, step, 0)
    for i in range(BLOCKS):
        r = lax.broadcasted_iota(jnp.int32, (NB, N), 0) + i * NB
        c = lax.broadcasted_iota(jnp.int32, (NB, N), 1)
        a = i * NB
        out_ref[a:a + NB, :] = jnp.where(r >= c, c_ref[a:a + NB, :], 0.0).astype(jnp.bfloat16)

    @pl.loop(1, PEERS)
    def _(k):
        copy_rows(0, k, peer(k // GROUP, k % GROUP), dp).wait_send()
        copy_rows(1, k, peer(k // GROUP, k % GROUP), dp).wait_send()
        copy_index(k, peer(k // GROUP, k % GROUP), dp).wait_send()


def inverse_factor(pair_scale, row_scale, rows_all, anchor, wanted, descriptors):
    dma = pltpu.SemaphoreType.DMA

    def sum_scratch(unit, piece):
        half = PLANE * unit
        return [
            pltpu.VMEM((NC * half, NB), F32),
            pltpu.VMEM((NC * half, NB), F32),
            pltpu.VMEM((half, NB), F32),
            pltpu.VMEM((half, NB), F32),
            pltpu.VMEM((PLANE, unit, NB), F32),
            pltpu.VMEM((NZ * piece, NB), F32),
            pltpu.VMEM((NZ, piece, NB), F32),
            pltpu.VMEM((NZ * piece, NB), F32),
            dma((8, PLANE)),
            dma((4, NZ)),
        ]

    return pl.pallas_call(
        functools.partial(factor_kernel, pair_scale, row_scale, rows_all),
        out_shape=[jax.ShapeDtypeStruct((N, N), jnp.bfloat16), jax.ShapeDtypeStruct((8, N), F32)],
        in_specs=[pl.BlockSpec(memory_space=pltpu.VMEM)] * 3,
        out_specs=[pl.BlockSpec(memory_space=pltpu.VMEM)] * 2,
        scratch_shapes=[
            pltpu.VMEM((2, PEERS, 2 * CAP, CUT // 2), jnp.bfloat16),
            pltpu.VMEM((2, PEERS, 2 * CAP, CUT // 2), jnp.bfloat16),
            pltpu.VMEM((PEERS, 1, NB), F32),
            pltpu.VMEM((PEERS * CAP, NB), F32),
            pltpu.VMEM((PEERS * CAP, N), jnp.bfloat16),
            pltpu.VMEM((PEERS * CAP, N), jnp.bfloat16),
            pltpu.VMEM((N, N), F32),
            pltpu.VMEM((N, N), F32),
            pltpu.VMEM((NB, NB), F32),
            dma((2, PEERS)), dma((2, PEERS)), dma((PEERS,)), dma((PEERS,)),
        ] + sum_scratch(UNIT_LEFT, PIECE_LEFT) + sum_scratch(UNIT_RIGHT, PIECE_RIGHT),
        compiler_params=pltpu.CompilerParams(
            collective_id=1, has_side_effects=True, vmem_limit_bytes=56 << 20
        ),
    )(anchor, wanted, descriptors)


def whiten_kernel(db_ref, mean_ref, inv_ref, out_ref):
    centered = (db_ref[...].astype(F32) - mean_ref[0:1, :]).astype(jnp.bfloat16)
    projected = lax.dot_general(
        centered, inv_ref[...], (((1,), (1,)), ((), ())), preferred_element_type=F32
    )
    energy = jnp.mean(projected * projected, axis=1, keepdims=True)
    out_ref[...] = (projected * lax.rsqrt(energy + norm_epsilon)).astype(jnp.bfloat16)


def whiten(database, col_mean, inverse):
    rows, width = database.shape
    tile = 256
    return pl.pallas_call(
        whiten_kernel,
        grid=(rows // tile,),
        out_shape=jax.ShapeDtypeStruct((rows, width), jnp.bfloat16),
        in_specs=[
            pl.BlockSpec((tile, width), lambda i: (i, 0)),
            pl.BlockSpec((8, width), lambda i: (0, 0)),
            pl.BlockSpec((width, width), lambda i: (0, 0)),
        ],
        out_specs=pl.BlockSpec((tile, width), lambda i: (i, 0)),
        compiler_params=pltpu.CompilerParams(vmem_limit_bytes=40 << 20),
    )(database, col_mean, inverse)


def shards(descriptors, database, anchor_row, partner_row, block_counts):
    local_rows = descriptors.shape[0]
    peer_count = partner_row.shape[1]
    slot_count = partner_row.shape[2]
    devices = lax.axis_size("dp") * lax.axis_size("mp")
    pairs_all = PAIRS_DEV * devices
    rows_all = local_rows * devices
    slot_iota = lax.broadcasted_iota(jnp.int32, (peer_count, slot_count), 1)
    live_slots = slot_iota < block_counts[0][:, None]
    wanted = jnp.where(live_slots, partner_row[0], -1).astype(F32)
    wanted = jnp.pad(wanted, ((0, 0), (0, NB - slot_count)))[:, None, :]
    anchor = jnp.where(live_slots, anchor_row[0], -1).astype(F32).reshape(-1, 1)
    inverse, col_mean = inverse_factor(
        1.0 / pairs_all,
        shrink_weight / rows_all,
        rows_all,
        jnp.broadcast_to(anchor, (peer_count * slot_count, NB)),
        wanted,
        descriptors,
    )
    return whiten(database, col_mean, inverse)


def solution(mesh):
    placed = (
        P(("dp", "mp"), None),
        P(("dp", "mp"), None),
        P(("dp", "mp"), None, None),
        P(("dp", "mp"), None, None),
        P(("dp", "mp"), None),
    )
    return jax.shard_map(
        shards, mesh=mesh, in_specs=placed, out_specs=P(("dp", "mp"), None), check_vma=False
    )
```

time: 484 us -> 196 us (0.40)
  waiting for transfers between devices: 254 us -> 0 us
  Pallas kernels: 78.7 us -> 186 us
  blocking collectives: 77 us -> 0 us
  starting transfers between devices: 23.6 us -> 0 us
  between operations: 13.5 us -> 0.04 us
  matrix products: 13.4 us -> 0 us
  local copies, waits for them, and re-layouts: 17.5 us -> 8.05 us
    psum x1 -> x0, waiting for transfers between devices: 187 us -> none  [shards(): summed, col_total = lax.psum((partial_sum, col_sum), ('dp', 'mp'))]
    pallas_call x1, Pallas kernels: 71 us -> 179 us  [inverse_factor(): pl.pallas_call(functools.partial(factor_kernel, pair_scale, row_scale, ro...]
    psum x1 -> x0, blocking collectives: 77 us -> none  [shards(): summed, col_total = lax.psum((partial_sum, col_sum), ('dp', 'mp'))]
    all_to_all x2 -> x0, waiting for transfers between devices: 67.2 us -> none  [the longest x1 67.2 us: shards(): lax.all_to_all(anchors, 'dp', split_axis=0, concat_axis=0, tiled=True)]
    all_to_all x2 -> x0, starting transfers between devices: 23.6 us -> none  [the longest x1 13 us: shards(): lax.all_to_all(wanted, 'dp', split_axis=0, concat_axis=0, tiled=True)]
    gather x2 -> x0, local copies, waits for them, and re-layouts: 15.4 us -> none  [the longest x1 9.65 us: shards(): descriptors.at[anchor_row[0].reshape(-1)].get(mode='promise_in_bounds')]
    dot_general x2 -> x0, matrix products: 13.4 us -> none  [the longest x1 8.97 us: shards(): lax.dot_general(pair_flat, pair_flat, contract_rows, preferred_element_ty...]
  transfers between devices with their start and end apart: 3 -> 0, of which waited for: 2 -> 0; matrix products, arithmetic and copies ran while one was open for 4% -> 0% of each run, Pallas kernels for 0% -> 0%
where the time goes in v4:
time: 196 us
  Pallas kernels  186 us (95%)
  local copies, waits for them, and re-layouts  8.05 us (4%)
    pallas_call x1, Pallas kernels, inverse_factor(): pl.pallas_call(functools.partial(factor_kernel, pair_scale, row_scale, ro...  179 us
    pallas_call x1, Pallas kernels, whiten(): pl.pallas_call(whiten_kernel, grid=(rows // tile,), out_shape=jax.ShapeDt...  7.63 us
    unnamed x8, local copies, waits for them, and re-layouts  6.11 us

profile of v4, /device:TPU:1, one launch (start us, length us, event | category | flops | bytes accessed | tf_op | source)
XLA Modules:
  0.0 195.8 jit_solution(10859250237475204906)
XLA Ops:
  0.0 0.7 iota_compare_fusion
  0.7 0.1 lt.20
  0.8 0.8 copy.7
  1.6 0.1 squeeze.6
  1.7 0.8 copy.8
  2.5 0.7 fusion
  3.2 0.6 pad.4
  3.9 1.1 broadcast_in_dim.16.anchor_ref
  5.0 178.6 %shard_map.55 = (bf16[1024,1024]{1,0:T(8,128)(2,1)}, f32[8,1024]{1,0:T(8,128)}) custom-call(f32[1536,128]{1,0:T(8,128)} %broadcast_in_dim.16.anchor_ref, f32[64,1,128]{2,1,0:T(1,128)} %bitcast.6, bf16[1024,1024]{1,0:T(8,128)(2,1)} %desc_ref.1), custom_call_target="tpu_custom_call" | custom-call | tf_op jit(solution)/shard_map/pallas_call | solution.py:542
  183.6 0.0 copy-start
  183.6 2.2 %copy-done = bf16[2048,1024]{1,0:T(8,128)(2,1)S(1)} copy-done((bf16[2048,1024]{1,0:T(8,128)(2,1)S(1)}, bf16[2048,1024]{1,0:T(8,128)(2,1)}, u32[]{:S(2)}) %copy-start) | copy-done | bytes 4194328
  185.8 0.0 copy-start.1
  185.8 1.6 copy-done.1
  187.4 0.0 copy-start.2
  187.4 0.8 copy-done.2
  188.1 7.6 %shard_map.56 = bf16[2048,1024]{1,0:T(8,128)(2,1)} custom-call(bf16[2048,1024]{1,0:T(8,128)(2,1)S(1)} %copy-done, f32[8,1024]{1,0:T(8,128)S(1)} %copy-done.2, bf16[1024,1024]{1,0:T(8,128)(2,1)S(1)} %copy-done.1), custom_call_target="tpu_custom_call" | custom-call | tf_op jit(solution)/shard_map/pallas_call | solution.py:577
  (1 shorter events, 0.0 us)
Async XLA Ops:
  183.6 2.2 %copy-start = (bf16[2048,1024]{1,0:T(8,128)(2,1)S(1)}, bf16[2048,1024]{1,0:T(8,128)(2,1)}, u32[]{:S(2)}) copy-start(bf16[2048,1024]{1,0:T(8,128)(2,1)} %db_ref.1) | copy-start | bytes 12582916
  185.8 1.6 copy-start.1
  187.4 0.8 copy-start.2

commit v5 on v4

--- a/solution.py
+++ b/solution.py
@@ -113,6 +113,14 @@
     return jnp.concatenate(parts, axis=1)
 
 
+def rem(a, b):
+    return a % b if isinstance(a, int) else lax.rem(a, b)
+
+
+def div(a, b):
+    return a // b if isinstance(a, int) else lax.div(a, b)
+
+
 def rows_at(base, count):
     return pl.ds(pl.multiple_of(base, 8), count)
 
@@ -123,31 +131,31 @@
         self.p, self.out, self.half, self.r0, self.r1 = p_ref, out_ref, half, r0, r1
         self.zb, self.r2, self.gz, self.near, self.far = zb, r2, gz, near, far
         dp, self.y = lax.axis_index("dp"), lax.axis_index("mp")
-        self.core, self.z, self.x = dp % NC, (dp // NC) % NZ, dp // (NC * NZ)
+        self.core, self.z, self.x = rem(dp, NC), rem(div(dp, NC), NZ), div(dp, NC * NZ)
         self.sibling = (dp + 1 - 2 * self.core, self.y)
         self.mine = self.x * NY + self.y
 
     def plane(self, o):
-        return (self.x + o // NY) % NX, (self.y + o % NY) % NY
+        return rem(self.x + div(o, NY), NX), rem(self.y + rem(o, NY), NY)
 
     def plane_from(self, o):
-        return (self.x + NX - o // NY) % NX, (self.y + NY - o % NY) % NY
+        return rem(self.x + NX - div(o, NY), NX), rem(self.y + NY - rem(o, NY), NY)
 
     def plane_id(self, o):
         tx, ty = self.plane(o)
         return ((tx * NZ + self.z) * NC + self.core, ty)
 
     def line_id(self, o):
-        return ((self.x * NZ + (self.z + o) % NZ) * NC + self.core, self.y)
+        return ((self.x * NZ + rem(self.z + o, NZ)) * NC + self.core, self.y)
 
     def near_copy(self, pair, o, src, dst, target):
         return pltpu.make_async_remote_copy(
-            src_ref=src, dst_ref=dst, send_sem=self.near.at[2 * pair, o], recv_sem=self.near.at[2 * pair + 1, o],
+            src_ref=src, dst_ref=dst, send_sem=self.near.at[2 * pair, 0], recv_sem=self.near.at[2 * pair + 1, o],
             device_id=target, device_id_type=MESH)
 
-    def far_copy(self, pair, o, src, dst, target):
+    def far_copy(self, pair, src, dst, target):
         return pltpu.make_async_remote_copy(
-            src_ref=src, dst_ref=dst, send_sem=self.far.at[2 * pair, o], recv_sem=self.far.at[2 * pair + 1, o],
+            src_ref=src, dst_ref=dst, send_sem=self.far.at[2 * pair], recv_sem=self.far.at[2 * pair + 1],
             device_id=target, device_id_type=MESH)
 
     def unit_at(self, o):
@@ -160,15 +168,15 @@
         return self.near_copy(0, o, src, self.r0.at[rows_at(at, self.unit)], self.sibling)
 
     def copy1(self, o):
-        return self.near_copy(1, o, self.half.at[rows_at(self.unit_at(o), self.unit)], self.r1.at[o], self.plane_id(o))
+        return self.near_copy(1, 0, self.half.at[rows_at(self.unit_at(o), self.unit)], self.r1.at[o], self.plane_id(o))
 
     def copy2(self, o):
-        src = self.zb.at[rows_at(((self.z + o) % NZ) * self.piece, self.piece)]
-        return self.far_copy(0, o, src, self.r2.at[o], self.line_id(o))
+        src = self.zb.at[rows_at((rem(self.z + o, NZ)) * self.piece, self.piece)]
+        return self.far_copy(0, src, self.r2.at[o], self.line_id(o))
 
     def copy3(self, o, owner):
         part = self.gz.at[rows_at(owner * self.piece, self.piece)]
-        return self.far_copy(1, o, part, part, self.line_id(o))
+        return self.far_copy(1, part, part, self.line_id(o))
 
     def copy4(self, o, owner):
         dst = self.out.at[rows_at(self.core * self.half_rows + owner * self.unit, self.unit)]
@@ -177,7 +185,7 @@
     def copy5(self, o, which):
         tx, ty = self.plane_from(o)
         part = self.out.at[rows_at(which * self.half_rows + (tx * NY + ty) * self.unit, self.unit)]
-        return self.near_copy(3, o, part, part, self.sibling)
+        return self.near_copy(3, 0, part, part, self.sibling)
 
     def to_sibling(self):
         @pl.loop(0, PLANE)
@@ -202,30 +210,31 @@
         self.zb[0:self.unit, :] = own + self.r0[rows_at(at, self.unit), :]
 
     def to_line(self):
-        @pl.loop(1, PLANE)
-        def _(o):
-            self.copy1(o).wait_recv()
-            self.zb[0:self.unit, :] = self.zb[0:self.unit, :] + self.r1[o]
+        got = self.r1.at[pl.ds(1, PLANE - 1)]
+        self.near_copy(1, 0, got, got, self.sibling).wait_recv()
+        total = self.zb[0:self.unit, :]
+        for o in range(1, PLANE):
+            total = total + self.r1[o]
+        self.zb[0:self.unit, :] = total
 
         @pl.loop(1, NZ)
         def _(o):
             self.copy2(o).start()
 
         own = rows_at(self.z * self.piece, self.piece)
-        self.gz[own, :] = self.zb[own, :]
-
-        @pl.loop(1, NZ)
-        def _(o):
-            self.copy2(o).wait_recv()
-            self.gz[own, :] = self.gz[own, :] + self.r2[o]
+        got = self.r2.at[pl.ds(1, NZ - 1)]
+        self.far_copy(0, got, got, self.sibling).wait_recv()
+        total = self.zb[own, :]
+        for o in range(1, NZ):
+            total = total + self.r2[o]
+        self.gz[own, :] = total
 
         @pl.loop(1, NZ)
         def _(o):
             self.copy3(o, self.z).start()
 
-        @pl.loop(1, NZ)
-        def _(o):
-            self.copy3(o, (self.z + NZ - o) % NZ).wait_recv()
+        got = self.gz.at[pl.ds(0, (NZ - 1) * self.piece)]
+        self.far_copy(1, got, got, self.sibling).wait_recv()
 
         @pl.loop(1, PLANE)
         def _(o):
@@ -241,63 +250,67 @@
             self.copy4(o, tx * NY + ty).wait_recv()
             self.copy5(o, self.core).start()
 
-        @pl.loop(0, PLANE)
-        def _(o):
-            self.copy5(o, 1 - self.core).wait_recv()
-            self.copy5(o, self.core).wait_send()
-            self.copy0(o).wait_send()
-
-        @pl.loop(1, PLANE)
-        def _(o):
-            self.copy1(o).wait_send()
-            self.copy4(o, self.mine).wait_send()
-
-        @pl.loop(1, NZ)
-        def _(o):
-            self.copy2(o).wait_send()
-            self.copy3(o, self.z).wait_send()
+        got = self.out.at[pl.ds(0, self.half_rows)]
+        self.near_copy(3, 0, got, got, self.sibling).wait_recv()
+
+    def drain(self):
+        whole = self.p.at[pl.ds(0, self.half_rows)]
+        others = self.p.at[pl.ds(0, self.half_rows - self.unit)]
+        line = self.zb.at[pl.ds(0, (NZ - 1) * self.piece)]
+        self.near_copy(0, 0, whole, whole, self.sibling).wait_send()
+        self.near_copy(1, 0, others, others, self.sibling).wait_send()
+        self.far_copy(0, line, line, self.sibling).wait_send()
+        self.far_copy(1, line, line, self.sibling).wait_send()
+        self.near_copy(2, 0, others, others, self.sibling).wait_send()
+        self.near_copy(3, 0, whole, whole, self.sibling).wait_send()
 
 
 def factor_kernel(pair_scale, row_scale, rows_all, anchor_ref, wanted_ref, desc_ref, out_ref, mean_ref,
                   sbuf, rbuf, windex, wcol, part_ref, diff_ref, gram_ref, c_ref, t_ref, s0, q0, s1, q1,
                   *sums):
     dp, y = lax.axis_index("dp"), lax.axis_index("mp")
-    core, z, x = dp % NC, (dp // NC) % NZ, dp // (NC * NZ)
+    core, z, x = rem(dp, NC), rem(div(dp, NC), NZ), div(dp, NC * NZ)
     left = Sum(UNIT_LEFT, PIECE_LEFT, *sums[:10])
     right = Sum(UNIT_RIGHT, PIECE_RIGHT, *sums[10:])
 
     def peer(ox, o):
-        return ((x + ox) % NX) * GROUP + ((z + o // NC) % NZ) * NC + (core + o % NC) % NC
-
-    def peer_from(ox, o):
-        return ((x + NX - ox) % NX) * GROUP + ((z + NZ - o // NC) % NZ) * NC + (core + NC - o % NC) % NC
-
-    def copy_rows(part, slot, target, owner):
+        return rem(x + ox, NX) * GROUP + rem(z + div(o, NC), NZ) * NC + rem(core + rem(o, NC), NC)
+
+    def copy_rows(part, ox, target):
         return pltpu.make_async_remote_copy(
-            src_ref=sbuf.at[part, target], dst_ref=rbuf.at[part, owner], send_sem=s0.at[part, slot],
-            recv_sem=q0.at[part, slot], device_id=(target, y), device_id_type=MESH)
-
-    def copy_index(slot, target, owner):
+            src_ref=sbuf.at[part, target], dst_ref=rbuf.at[part, dp], send_sem=s0.at[part],
+            recv_sem=q0.at[part, ox], device_id=(target, y), device_id_type=MESH)
+
+    def rows_of(part, ox, count):
         return pltpu.make_async_remote_copy(
-            src_ref=wanted_ref.at[target], dst_ref=windex.at[owner], send_sem=s1.at[slot], recv_sem=q1.at[slot],
+            src_ref=sbuf.at[part, pl.ds(0, count)], dst_ref=rbuf.at[part, pl.ds(0, count)], send_sem=s0.at[part],
+            recv_sem=q0.at[part, ox], device_id=left.sibling, device_id_type=MESH)
+
+    def copy_index(target):
+        return pltpu.make_async_remote_copy(
+            src_ref=wanted_ref.at[target], dst_ref=windex.at[dp], send_sem=s1.at[0], recv_sem=q1.at[0],
             device_id=(target, y), device_id_type=MESH)
+
+    indices = pltpu.make_async_remote_copy(
+        src_ref=wanted_ref.at[pl.ds(0, PEERS - 1)], dst_ref=windex.at[pl.ds(0, PEERS - 1)], send_sem=s1.at[0],
+        recv_sem=q1.at[0], device_id=left.sibling, device_id_type=MESH)
 
     barrier = pltpu.get_barrier_semaphore()
 
     @pl.loop(1, PEERS)
     def _(k):
-        pl.semaphore_signal(barrier, inc=1, device_id=(peer(k // GROUP, k % GROUP), y), device_id_type=MESH)
+        pl.semaphore_signal(barrier, inc=1, device_id=(peer(div(k, GROUP), rem(k, GROUP)), y), device_id_type=MESH)
 
     @pl.loop(1, PLANE)
     def _(o):
-        @pl.when(o % NY != 0)
+        @pl.when(rem(o, NY) != 0)
         def _():
             pl.semaphore_signal(barrier, inc=1, device_id=left.plane_id(o), device_id_type=MESH)
 
     rows_x = GROUP * CAP
 
     def gather(ox):
-        group = (x + ox) % NX
+        group = rem(x + ox, NX)
         base = group * rows_x
         for h in range(2):
             count = rows_x // 2
@@ -317,17 +330,15 @@
     def _(ox):
         @pl.loop(0, GROUP)
         def _(o):
-            slot = ox * GROUP + o
-
-            @pl.when(slot > 0)
+            @pl.when(ox * GROUP + o > 0)
             def _():
-                copy_rows(0, slot, peer(ox, o), dp).start()
+                copy_rows(0, ox, peer(ox, o)).start()
 
         @pl.when(ox == 0)
         def _():
             @pl.loop(1, PEERS)
             def _(k):
-                copy_index(k, peer(k // GROUP, k % GROUP), dp).start()
+                copy_index(peer(div(k, GROUP), rem(k, GROUP))).start()
 
         @pl.when(ox < NX - 1)
         def _():
@@ -335,7 +346,7 @@
 
     @pl.loop(1, PEERS)
     def _(k):
-        copy_rows(1, k, peer(k // GROUP, k % GROUP), dp).start()
+        copy_rows(1, div(k, GROUP), peer(div(k, GROUP), rem(k, GROUP))).start()
 
     tile = 256
     for i in range(0, N, tile):
@@ -352,10 +363,7 @@
 
     windex[dp] = wanted_ref[dp]
 
-    @pl.loop(1, PEERS)
-    def _(k):
-        copy_index(k, peer(k // GROUP, k % GROUP), peer_from(k // GROUP, k % GROUP)).wait_recv()
-
+    indices.wait_recv()
     turned = windex[...].reshape(PEERS, NB)
     turned = jnp.concatenate([turned, jnp.zeros((NB - PEERS, NB), F32)], axis=0).T
     for p in range(PEERS):
@@ -377,16 +385,16 @@
 
         @pl.loop(0, NX)
         def _(ox):
-            group = (x + NX - ox) % NX
+            group = rem(x + NX - ox, NX)
             start = ox * rows_x
 
-            @pl.loop(0, GROUP)
-            def _(o):
-                slot = ox * GROUP + o
-
-                @pl.when(slot > 0)
-                def _():
-                    copy_rows(part, slot, peer(ox, o), peer_from(ox, o)).wait_recv()
+            @pl.when(ox == 0)
+            def _():
+                rows_of(part, ox, GROUP - 1).wait_recv()
+
+            @pl.when(ox > 0)
+            def _():
+                rows_of(part, ox, GROUP).wait_recv()
 
             @pl.loop(0, GROUP // 2)
             def _(m):
@@ -446,6 +454,10 @@
         @pl.when(k == 1)
         def _():
             right.to_plane()
+            left.drain()
+            rows_of(0, 0, PEERS - 1).wait_send()
+            rows_of(1, 0, PEERS - 1).wait_send()
+            indices.wait_send()
 
         @pl.when(k == 3)
         def _():
@@ -514,11 +526,7 @@
         a = i * NB
         out_ref[a:a + NB, :] = jnp.where(r >= c, c_ref[a:a + NB, :], 0.0).astype(jnp.bfloat16)
 
-    @pl.loop(1, PEERS)
-    def _(k):
-        copy_rows(0, k, peer(k // GROUP, k % GROUP), dp).wait_send()
-        copy_rows(1, k, peer(k // GROUP, k % GROUP), dp).wait_send()
-        copy_index(k, peer(k // GROUP, k % GROUP), dp).wait_send()
+    right.drain()
 
 
 def inverse_factor(pair_scale, row_scale, rows_all, anchor, wanted, descriptors):
@@ -536,7 +544,7 @@
             pltpu.VMEM((NZ, piece, NB), F32),
             pltpu.VMEM((NZ * piece, NB), F32),
             dma((8, PLANE)),
-            dma((4, NZ)),
+            dma((4,)),
         ]
 
     return pl.pallas_call(
@@ -554,7 +562,7 @@
             pltpu.VMEM((N, N), F32),
             pltpu.VMEM((N, N), F32),
             pltpu.VMEM((NB, NB), F32),
-            dma((2, PEERS)), dma((2, PEERS)), dma((PEERS,)), dma((PEERS,)),
+            dma((2,)), dma((2, NX)), dma((1,)), dma((1,)),
         ] + sum_scratch(UNIT_LEFT, PIECE_LEFT) + sum_scratch(UNIT_RIGHT, PIECE_RIGHT),
         compiler_params=pltpu.CompilerParams(
             collective_id=1, has_side_effects=True, vmem_limit_bytes=56 << 20
@@ -580,8 +588,8 @@
         out_shape=jax.ShapeDtypeStruct((rows, width), jnp.bfloat16),
         in_specs=[
             pl.BlockSpec((tile, width), lambda i: (i, 0)),
-            pl.BlockSpec((8, width), lambda i: (0, 0)),
-            pl.BlockSpec((width, width), lambda i: (0, 0)),
+            pl.BlockSpec(memory_space=pltpu.VMEM),
+            pl.BlockSpec(memory_space=pltpu.VMEM),
         ],
         out_specs=pl.BlockSpec((tile, width), lambda i: (i, 0)),
         compiler_params=pltpu.CompilerParams(vmem_limit_bytes=40 << 20),

time: 196 us -> 191 us (0.974)
  Pallas kernels: 186 us -> 181 us
    pallas_call x1, Pallas kernels: 179 us -> 173 us  [inverse_factor(): pl.pallas_call(functools.partial(factor_kernel, pair_scale, row_scale, ro...]
where the time goes in v5:
time: 191 us
  Pallas kernels  181 us (95%)
  local copies, waits for them, and re-layouts  8.05 us (4%)
    pallas_call x1, Pallas kernels, inverse_factor(): pl.pallas_call(functools.partial(factor_kernel, pair_scale, row_scale, ro...  173 us
    pallas_call x1, Pallas kernels, whiten(): pl.pallas_call(whiten_kernel, grid=(rows // tile,), out_shape=jax.ShapeDt...  7.61 us
    unnamed x8, local copies, waits for them, and re-layouts  6.11 us

profile of v5, /device:TPU:1, one launch (start us, length us, event | category | flops | bytes accessed | tf_op | source)
XLA Modules:
  0.0 190.6 jit_solution(57100880735453838)
XLA Ops:
  0.0 0.7 iota_compare_fusion
  0.7 0.1 lt.20
  0.8 0.8 copy.7
  1.6 0.1 squeeze.6
  1.7 0.8 copy.8
  2.5 0.7 fusion
  3.2 0.6 pad.4
  3.9 1.1 broadcast_in_dim.16.anchor_ref
  5.0 173.4 %shard_map.55 = (bf16[1024,1024]{1,0:T(8,128)(2,1)}, f32[8,1024]{1,0:T(8,128)}) custom-call(f32[1536,128]{1,0:T(8,128)} %broadcast_in_dim.16.anchor_ref, f32[64,1,128]{2,1,0:T(1,128)} %bitcast.6, bf16[1024,1024]{1,0:T(8,128)(2,1)} %desc_ref.1), custom_call_target="tpu_custom_call" | custom-call | tf_op jit(solution)/shard_map/pallas_call | solution.py:550
  178.4 0.0 copy-start
  178.4 2.2 %copy-done = bf16[2048,1024]{1,0:T(8,128)(2,1)S(1)} copy-done((bf16[2048,1024]{1,0:T(8,128)(2,1)S(1)}, bf16[2048,1024]{1,0:T(8,128)(2,1)}, u32[]{:S(2)}) %copy-start) | copy-done | bytes 4194328
  180.6 0.0 copy-start.1
  180.6 1.6 copy-done.1
  182.2 0.0 copy-start.2
  182.2 0.8 copy-done.2
  182.9 7.6 %shard_map.56 = bf16[2048,1024]{1,0:T(8,128)(2,1)} custom-call(bf16[2048,1024]{1,0:T(8,128)(2,1)S(1)} %copy-done, f32[8,1024]{1,0:T(8,128)S(1)} %copy-done.2, bf16[1024,1024]{1,0:T(8,128)(2,1)S(1)} %copy-done.1), custom_call_target="tpu_custom_call" | custom-call | tf_op jit(solution)/shard_map/pallas_call | solution.py:585
  (1 shorter events, 0.0 us)
Async XLA Ops:
  178.4 2.2 %copy-start = (bf16[2048,1024]{1,0:T(8,128)(2,1)S(1)}, bf16[2048,1024]{1,0:T(8,128)(2,1)}, u32[]{:S(2)}) copy-start(bf16[2048,1024]{1,0:T(8,128)(2,1)} %db_ref.1) | copy-start | bytes 12582916
  180.6 1.6 copy-start.1
  182.2 0.8 copy-start.2

commit v6 on v5

--- a/solution.py
+++ b/solution.py
@@ -314,7 +314,7 @@
         base = group * rows_x
         for h in range(2):
             count = rows_x // 2
-            index = anchor_ref[pl.ds(pl.multiple_of(base + h * count, count), count), :]
+            index = wcol[pl.ds(pl.multiple_of(base + h * count, count), count), :]
             found = jnp.dot(one_hot_rows(index, count), desc_ref[...], preferred_element_type=F32)
             for p in range(GROUP // 2):
                 block = found[p * CAP:(p + 1) * CAP, :]
@@ -323,6 +323,12 @@
                     halves = jnp.concatenate([block[:, a:a + CUT // 2], block[:, a + CUT // 2:a + CUT]], axis=0)
                     sbuf[part, group * GROUP + h * (GROUP // 2) + p] = halves.astype(jnp.bfloat16)
 
+    def turn(rows):
+        turned = jnp.concatenate([rows.reshape(PEERS, NB), jnp.zeros((NB - PEERS, NB), F32)], axis=0).T
+        for p in range(PEERS):
+            wcol[p * CAP:(p + 1) * CAP, :] = jnp.broadcast_to(turned[0:CAP, p:p + 1], (CAP, NB))
+
+    turn(anchor_ref[...])
     gather(0)
     pl.semaphore_wait(barrier, PEERS - 1 + PLANE - NX)
 
@@ -344,9 +350,10 @@
         def _():
             gather(ox + 1)
 
-    @pl.loop(1, PEERS)
-    def _(k):
-        copy_rows(1, div(k, GROUP), peer(div(k, GROUP), rem(k, GROUP))).start()
+    def send_right(ox):
+        @pl.loop(0 if ox else 1, GROUP)
+        def _(o):
+            copy_rows(1, ox, peer(ox, o)).start()
 
     tile = 256
     for i in range(0, N, tile):
@@ -364,10 +371,7 @@
     windex[dp] = wanted_ref[dp]
 
     indices.wait_recv()
-    turned = windex[...].reshape(PEERS, NB)
-    turned = jnp.concatenate([turned, jnp.zeros((NB - PEERS, NB), F32)], axis=0).T
-    for p in range(PEERS):
-        wcol[p * CAP:(p + 1) * CAP, :] = jnp.broadcast_to(turned[0:CAP, p:p + 1], (CAP, NB))
+    turn(windex[...])
 
     count = 192
 
@@ -395,6 +399,11 @@
             @pl.when(ox > 0)
             def _():
                 rows_of(part, ox, GROUP).wait_recv()
+
+            if part == 0:
+                @pl.when(ox == 2)
+                def _():
+                    send_right(0)
 
             @pl.loop(0, GROUP // 2)
             def _(m):
@@ -429,10 +438,13 @@
     for r, c, at in segments(LEFT, DATA_LEFT, UNIT_LEFT):
         left.p[at:at + 8, :] = gram_ref[r:r + 8, c:c + NB]
     left.to_sibling()
+    send_right(1)
     c_ref[...] = jnp.zeros((N, N), F32)
     mean_ref[...] = jnp.zeros((8, N), F32)
     left.to_plane()
+    send_right(2)
     left.to_line()
+    send_right(3)
     left.finish()
     means = left.out[DATA_LEFT:UNIT_LEFT, :] * (1.0 / rows_all)
     for i in range(BLOCKS):
@@ -572,11 +584,17 @@
 
 def whiten_kernel(db_ref, mean_ref, inv_ref, out_ref):
     centered = (db_ref[...].astype(F32) - mean_ref[0:1, :]).astype(jnp.bfloat16)
-    projected = lax.dot_general(
-        centered, inv_ref[...], (((1,), (1,)), ((), ())), preferred_element_type=F32
-    )
-    energy = jnp.mean(projected * projected, axis=1, keepdims=True)
-    out_ref[...] = (projected * lax.rsqrt(energy + norm_epsilon)).astype(jnp.bfloat16)
+    block = 2 * NB
+    parts = []
+    energy = 0.0
+    for a in range(0, N, block):
+        b = a + block
+        part = lax.dot_general(centered[:, :b], inv_ref[a:b, :b], (((1,), (1,)), ((), ())), preferred_element_type=F32)
+        energy = energy + jnp.sum(part * part, axis=1, keepdims=True)
+        parts.append(part)
+    scale = lax.rsqrt(energy * (1.0 / N) + norm_epsilon)
+    for i, part in enumerate(parts):
+        out_ref[:, i * block:(i + 1) * block] = (part * scale).astype(jnp.bfloat16)
 
 
 def whiten(database, col_mean, inverse):
@@ -588,11 +606,11 @@
         out_shape=jax.ShapeDtypeStruct((rows, width), jnp.bfloat16),
         in_specs=[
             pl.BlockSpec((tile, width), lambda i: (i, 0)),
-            pl.BlockSpec(memory_space=pltpu.VMEM),
-            pl.BlockSpec(memory_space=pltpu.VMEM),
+            pl.BlockSpec((8, width), lambda i: (0, 0)),
+            pl.BlockSpec((width, width), lambda i: (0, 0)),
         ],
         out_specs=pl.BlockSpec((tile, width), lambda i: (i, 0)),
-        compiler_params=pltpu.CompilerParams(vmem_limit_bytes=40 << 20),
+        compiler_params=pltpu.CompilerParams(vmem_limit_bytes=60 << 20),
     )(database, col_mean, inverse)
 
 
@@ -605,14 +623,14 @@
     rows_all = local_rows * devices
     slot_iota = lax.broadcasted_iota(jnp.int32, (peer_count, slot_count), 1)
     live_slots = slot_iota < block_counts[0][:, None]
-    wanted = jnp.where(live_slots, partner_row[0], -1).astype(F32)
-    wanted = jnp.pad(wanted, ((0, 0), (0, NB - slot_count)))[:, None, :]
-    anchor = jnp.where(live_slots, anchor_row[0], -1).astype(F32).reshape(-1, 1)
+    room = ((0, 0), (0, NB - slot_count))
+    wanted = jnp.pad(jnp.where(live_slots, partner_row[0], -1).astype(F32), room)[:, None, :]
+    anchor = jnp.pad(jnp.where(live_slots, anchor_row[0], -1).astype(F32), room)[:, None, :]
     inverse, col_mean = inverse_factor(
         1.0 / pairs_all,
         shrink_weight / rows_all,
         rows_all,
-        jnp.broadcast_to(anchor, (peer_count * slot_count, NB)),
+        anchor,
         wanted,
         descriptors,
     )

time: 191 us -> 187 us (0.979)
  local copies, waits for them, and re-layouts: 8.05 us -> 2.81 us
  Pallas kernels: 181 us -> 184 us
    unnamed x8 -> x2, local copies, waits for them, and re-layouts: 6.11 us -> 1.58 us
    pallas_call x1, Pallas kernels: 7.61 us -> 9.75 us  [whiten(): pl.pallas_call(whiten_kernel, grid=(rows // tile,), out_shape=jax.ShapeDt...]
where the time goes in v6:
time: 187 us
  Pallas kernels  184 us (98%)
  local copies, waits for them, and re-layouts  2.81 us (2%)
    pallas_call x1, Pallas kernels, inverse_factor(): pl.pallas_call(functools.partial(factor_kernel, pair_scale, row_scale, ro...  174 us
    pallas_call x1, Pallas kernels, whiten(): pl.pallas_call(whiten_kernel, grid=(rows // tile,), out_shape=jax.ShapeDt...  9.75 us

profile of v6, /device:TPU:1, one launch (start us, length us, event | category | flops | bytes accessed | tf_op | source)
XLA Modules:
  0.0 187.1 jit_solution(9070428244241448827)
XLA Ops:
  0.0 0.8 copy.6
  0.8 0.8 copy.7
  1.6 0.7 fusion
  2.3 0.6 pad.8
  2.9 0.6 pad.7
  3.5 173.8 %shard_map.55 = (bf16[1024,1024]{1,0:T(8,128)(2,1)}, f32[8,1024]{1,0:T(8,128)}) custom-call(f32[64,1,128]{2,1,0:T(1,128)} %bitcast.14, f32[64,1,128]{2,1,0:T(1,128)} %bitcast.13, bf16[1024,1024]{1,0:T(8,128)(2,1)} %desc_ref.1), custom_call_target="tpu_custom_call" | custom-call | tf_op jit(solution)/shard_map/pallas_call | solution.py:562
  177.4 9.7 %shard_map.56 = bf16[2048,1024]{1,0:T(8,128)(2,1)} custom-call(bf16[2048,1024]{1,0:T(8,128)(2,1)} %db_ref.1, f32[8,1024]{1,0:T(8,128)} %get-tuple-element.7.mean_ref, bf16[1024,1024]{1,0:T(8,128)(2,1)} %get-tuple-element.8.inv_ref), custom_call_target="tpu_custom_call" | custom-call | tf_op jit(solution)/shard_map/pallas_call | solution.py:603

commit v7 on v6

--- a/solution.py
+++ b/solution.py
@@ -438,13 +438,13 @@
     for r, c, at in segments(LEFT, DATA_LEFT, UNIT_LEFT):
         left.p[at:at + 8, :] = gram_ref[r:r + 8, c:c + NB]
     left.to_sibling()
-    send_right(1)
     c_ref[...] = jnp.zeros((N, N), F32)
     mean_ref[...] = jnp.zeros((8, N), F32)
     left.to_plane()
+    send_right(1)
     send_right(2)
+    send_right(3)
     left.to_line()
-    send_right(3)
     left.finish()
     means = left.out[DATA_LEFT:UNIT_LEFT, :] * (1.0 / rows_all)
     for i in range(BLOCKS):
@@ -463,7 +463,7 @@
     col = lax.broadcasted_iota(jnp.int32, (NB, NB), 1)
 
     def step(k, _):
-        @pl.when(k == 1)
+        @pl.when(k == 0)
         def _():
             right.to_plane()
             left.drain()
@@ -471,7 +471,7 @@
             rows_of(1, 0, PEERS - 1).wait_send()
             indices.wait_send()
 
-        @pl.when(k == 3)
+        @pl.when(k == 2)
         def _():
             right.to_line()
 

time: 187 us -> 182 us (0.973)
  Pallas kernels: 184 us -> 178 us
    pallas_call x1, Pallas kernels: 174 us -> 168 us  [inverse_factor(): pl.pallas_call(functools.partial(factor_kernel, pair_scale, row_scale, ro...]
where the time goes in v7:
time: 182 us; the launch traced here: 181 us
  Pallas kernels  178 us (98%)
  local copies, waits for them, and re-layouts  2.81 us (2%)
    pallas_call x1, Pallas kernels, inverse_factor(): pl.pallas_call(functools.partial(factor_kernel, pair_scale, row_scale, ro...  168 us
    pallas_call x1, Pallas kernels, whiten(): pl.pallas_call(whiten_kernel, grid=(rows // tile,), out_shape=jax.ShapeDt...  9.75 us

profile of v7, /device:TPU:1, one launch (start us, length us, event | category | flops | bytes accessed | tf_op | source)
XLA Modules:
  0.0 181.3 jit_solution(9666674911398942594)
XLA Ops:
  0.0 0.8 copy.6
  0.8 0.8 copy.7
  1.6 0.7 fusion
  2.3 0.6 pad.8
  2.9 0.6 pad.7
  3.5 168.0 %shard_map.55 = (bf16[1024,1024]{1,0:T(8,128)(2,1)}, f32[8,1024]{1,0:T(8,128)}) custom-call(f32[64,1,128]{2,1,0:T(1,128)} %bitcast.14, f32[64,1,128]{2,1,0:T(1,128)} %bitcast.13, bf16[1024,1024]{1,0:T(8,128)(2,1)} %desc_ref.1), custom_call_target="tpu_custom_call" | custom-call | tf_op jit(solution)/shard_map/pallas_call | solution.py:562
  171.6 9.7 %shard_map.56 = bf16[2048,1024]{1,0:T(8,128)(2,1)} custom-call(bf16[2048,1024]{1,0:T(8,128)(2,1)} %db_ref.1, f32[8,1024]{1,0:T(8,128)} %get-tuple-element.7.mean_ref, bf16[1024,1024]{1,0:T(8,128)(2,1)} %get-tuple-element.8.inv_ref), custom_call_target="tpu_custom_call" | custom-call | tf_op jit(solution)/shard_map/pallas_call | solution.py:603
